TPU v7x, 512 devices: a whole 4x8x8 slice. The times are simulated.
512 devices in a mesh: span: 16 (over z, x_hi), flow: 32 (over y, x_lo, core).
Axes of the slice: x: 4 (x_hi: 2, x_lo: 2; x = x_hi * 2 + x_lo), y: 8, z: 8, core: 2. Of those that a mesh axis runs over, the one named last changes fastest.
Arguments:
- rhs_fluid: float32 [6, 32, 256, 128], P(None, 'span', 'flow'), may hold values from -6 to 6
- rhs_solid: float32 [512, 128], P('span'), may hold values from -6 to 6
- blocks: float32 [6, 6, 32, 256, 128], P(None, None, 'span', 'flow')
- weights: float32 [6, 32, 256, 128], P(None, 'span', 'flow'), may hold values from 0.5 to 1.1
- kdiag: float32 [512, 128], P('span'), may hold values from 1 to 4
- wall_fluid: int32 [16, 32], P('span', 'flow'), may hold values from 0 to 15
- wall_solid: int32 [16, 32], P('span', 'flow'), may hold values from 0 to 31, each once within a row
- wall_coef: float32 [16, 32, 128], P('span', 'flow'), may hold values from 0.3 to 1.5
Outputs:
- x_fluid: float32 [6, 32, 256, 128], P(None, 'span', 'flow')
- x_solid: float32 [512, 128], P('span')
Inputs may be any that keep to these rules, and one draw needn't show every extreme that they name: `wall_fluid`: a local row a * 8 + b of the fluid tile of span index i and flow index q; rows may repeat. `wall_solid`: each row is a permutation of the 32 metal rows of band i.
All inputs are finite; a program needn't handle non-finite values.
Results may differ from a plain program's by a relative error of at most 0.0003.
Values sent between devices are 32-bit elements; how exact they have to be, the bound alone decides.
A program may use at most 64 MiB of HBM per device.

v0:
```python
import jax
import jax.numpy as jnp
from jax import lax
from jax.sharding import PartitionSpec as P

KRYLOV = 6


def extended(shard, sides, width):
    for axis, dim in sides:
        count, length = (lax.axis_size(axis), shard.shape[dim])
        up = [(i, (i + 1) % count) for i in range(count - 1)]
        down = [(j, i) for i, j in up]
        last = lax.slice_in_dim(shard, length - width, length, axis=dim)
        first = lax.slice_in_dim(shard, 0, width, axis=dim)
        before = lax.ppermute(last, axis, up)
        after = lax.ppermute(first, axis, down)
        shard = jnp.concatenate([before, shard, after], axis=dim)
    return shard


def least_squares(hess, beta, steps):
    cos_list, sin_list, upper = ([], [], [])
    rhs_g = [beta] + [jnp.float32(0.0) for _ in range(steps)]
    for j in range(steps):
        column = [hess[i][j] for i in range(j + 2)]
        for i in range(j):
            top = cos_list[i] * column[i] + sin_list[i] * column[i + 1]
            column[i + 1] = -sin_list[i] * column[i] + cos_list[i] * column[i + 1]
            column[i] = top
        radius = jnp.sqrt(column[j] * column[j] + column[j + 1] * column[j + 1])
        cos_now = column[j] / radius
        sin_now = column[j + 1] / radius
        column[j] = radius
        rhs_g[j + 1] = -sin_now * rhs_g[j]
        rhs_g[j] = cos_now * rhs_g[j]
        cos_list.append(cos_now)
        sin_list.append(sin_now)
        upper.append(column[: j + 1])
    coeffs = [None] * steps
    for j in range(steps - 1, -1, -1):
        total = rhs_g[j]
        for k in range(j + 1, steps):
            total = total - upper[k][j] * coeffs[k]
        coeffs[j] = total / upper[j][j]
    return coeffs


def shards(rhs_fluid, rhs_solid, blocks, weights, kdiag, wall_fluid, wall_solid, wall_coef):
    rows_a = rhs_fluid.shape[1]
    rows_b = rhs_fluid.shape[2]
    width = rhs_fluid.shape[3]
    cells = rows_a * rows_b
    band_rows = rhs_solid.shape[0]
    patch_rows = wall_fluid[0]
    patch_metal = wall_solid[0]
    coef = wall_coef[0]
    fluid_pick = (jnp.arange(cells, dtype=jnp.int32)[:, None] == patch_rows[None, :]).astype(
        jnp.float32
    )
    metal_pick = (jnp.arange(band_rows, dtype=jnp.int32)[:, None] == patch_metal[None, :]).astype(
        jnp.float32
    )
    first_flow = (lax.axis_index("flow") == 0).astype(jnp.float32)
    highest = lax.Precision.HIGHEST

    def local_inner(left, right):
        return jnp.sum(left[0] * right[0]) + first_flow * jnp.sum(left[1] * right[1])

    beta = jnp.sqrt(
        lax.psum(local_inner((rhs_fluid, rhs_solid), (rhs_fluid, rhs_solid)), ("span", "flow"))
    )
    basis = [(rhs_fluid / beta, rhs_solid / beta)]
    hess = [[jnp.float32(0.0) for _ in range(KRYLOV)] for _ in range(KRYLOV + 1)]
    for j in range(KRYLOV):
        field = basis[j][0]
        metal_u = basis[j][1]
        padded = extended(field, (("span", 1), ("flow", 2)), 1)
        local = jnp.einsum("fgabc,gabc->fabc", blocks, field, precision=highest)
        beside = weights[0][None] * padded[:, :-2, 1:-1] + weights[1][None] * padded[:, 2:, 1:-1]
        beside = (
            beside
            + weights[2][None] * padded[:, 1:-1, :-2]
            + weights[3][None] * padded[:, 1:-1, 2:]
        )
        beside = (
            beside
            + weights[4][None] * jnp.roll(field, 1, axis=3)
            + weights[5][None] * jnp.roll(field, -1, axis=3)
        )
        metal_at = jnp.dot(metal_pick.T, metal_u, precision=highest)
        inflow = jnp.dot(fluid_pick, coef * metal_at, precision=highest).reshape(
            rows_a, rows_b, width
        )
        image_f = (local - beside).at[5].add(-inflow)
        wall_vals = coef * jnp.dot(fluid_pick.T, field[5].reshape(cells, width), precision=highest)
        sink = lax.psum(jnp.dot(metal_pick, wall_vals, precision=highest), "flow")
        upad = extended(metal_u, (("span", 0),), 1)
        beside_all = (
            upad[:-2] + upad[2:] + jnp.roll(metal_u, 1, axis=1) + jnp.roll(metal_u, -1, axis=1)
        )
        image_s = (4.0 + kdiag) * metal_u - beside_all - sink
        image_f, image_s = (image_f, image_s)
        terms = jnp.stack([local_inner(basis[i], (image_f, image_s)) for i in range(j + 1)])
        values = lax.psum(terms, ("span", "flow"))
        for i in range(j + 1):
            image_f = image_f - values[i] * basis[i][0]
            image_s = image_s - values[i] * basis[i][1]
        rest = jnp.sqrt(
            lax.psum(local_inner((image_f, image_s), (image_f, image_s)), ("span", "flow"))
        )
        for i in range(j + 1):
            hess[i][j] = values[i]
        hess[j + 1][j] = rest
        basis.append((image_f / rest, image_s / rest))
    coeffs = least_squares(hess, beta, KRYLOV)
    x_fluid = jnp.zeros_like(rhs_fluid)
    x_solid = jnp.zeros_like(rhs_solid)
    for j in range(KRYLOV):
        x_fluid = x_fluid + coeffs[j] * basis[j][0]
        x_solid = x_solid + coeffs[j] * basis[j][1]
    return (x_fluid, x_solid)


def solution(mesh):
    in_specs = (
        P(None, "span", "flow", None),
        P("span", None),
        P(None, None, "span", "flow", None),
        P(None, "span", "flow", None),
        P("span", None),
        P("span", "flow"),
        P("span", "flow"),
        P("span", "flow", None),
    )
    out_specs = (P(None, "span", "flow", None), P("span", None))
    return jax.shard_map(shards, mesh=mesh, in_specs=in_specs, out_specs=out_specs, check_vma=False)
```

profile of v0, /device:TPU:1, one launch (start us, length us, event | category | flops | bytes accessed | tf_op | source)
XLA Modules:
  0.0 2140.4 jit_solution(9894139930378787865)
XLA Ops:
  4.7 106.1 %psum.133 = f32[]{:T(128)} all-reduce(f32[]{:T(128)S(6)} %add.455), channel_id=1, replica_groups=mesh['span'=16,'flow'=32] {'span','flow'}, use_global_device_ids=true, to_apply=%region_2.0 | all-reduce | flops 1 | bytes 8 | tf_op jit(solution)/shard_map/psum | solution.py:71
  128.6 101.7 %psum.134 = f32[32,128]{1,0:T(8,128)S(1)} all-reduce(f32[32,128]{1,0:T(8,128)S(1)} %broadcast_multiply_fusion.5), channel_id=1, replica_groups=mesh['span'=16,'flow'=32] {'flow'}, use_global_device_ids=true, to_apply=%region_4.5 | all-reduce | flops 4096 | bytes 32768 | tf_op jit(solution)/shard_map/psum | solution.py:97
  230.4 6.3 collective-permute-start.3
  241.8 96.7 %psum.135 = f32[]{:T(128)} all-reduce(f32[]{:T(128)S(6)} %add.466), channel_id=1, replica_groups=mesh['span'=16,'flow'=32] {'span','flow'}, use_global_device_ids=true, to_apply=%region_6.7 | all-reduce | flops 1 | bytes 8 | tf_op jit(solution)/shard_map/psum | solution.py:105
  342.3 95.3 %psum.136 = f32[]{:T(128)} all-reduce(f32[]{:T(128)S(6)} %add.467), channel_id=1, replica_groups=mesh['span'=16,'flow'=32] {'span','flow'}, use_global_device_ids=true, to_apply=%region_9.10 | all-reduce | flops 1 | bytes 8 | tf_op jit(solution)/shard_map/psum | solution.py:110
  456.0 103.9 %psum.137 = f32[32,128]{1,0:T(8,128)S(1)} all-reduce(f32[32,128]{1,0:T(8,128)S(1)} %broadcast_multiply_fusion.4), channel_id=1, replica_groups=mesh['span'=16,'flow'=32] {'flow'}, use_global_device_ids=true, to_apply=%region_11.12 | all-reduce | flops 4096 | bytes 32768 | tf_op jit(solution)/shard_map/psum | solution.py:97
  560.0 6.3 collective-permute-start.9
  572.6 97.2 %psum.138 = f32[2]{0:T(128)S(1)} all-reduce(f32[2]{0:T(128)S(1)} %pad_maximum_fusion.78), channel_id=1, replica_groups=mesh['span'=16,'flow'=32] {'span','flow'}, use_global_device_ids=true, to_apply=%region_15.16 | all-reduce | flops 2 | bytes 16 | tf_op jit(solution)/shard_map/psum | solution.py:105
  675.5 94.4 %psum.139 = f32[]{:T(128)} all-reduce(f32[]{:T(128)S(6)} %add.482), channel_id=1, replica_groups=mesh['span'=16,'flow'=32] {'span','flow'}, use_global_device_ids=true, to_apply=%region_18.19 | all-reduce | flops 1 | bytes 8 | tf_op jit(solution)/shard_map/psum | solution.py:110
  787.6 104.2 %psum.140 = f32[32,128]{1,0:T(8,128)S(1)} all-reduce(f32[32,128]{1,0:T(8,128)S(1)} %broadcast_multiply_fusion.3), channel_id=1, replica_groups=mesh['span'=16,'flow'=32] {'flow'}, use_global_device_ids=true, to_apply=%region_20.21 | all-reduce | flops 4096 | bytes 32768 | tf_op jit(solution)/shard_map/psum | solution.py:97
  891.8 6.3 collective-permute-start.15
  905.7 97.2 %psum.141 = f32[3]{0:T(128)S(1)} all-reduce(f32[3]{0:T(128)S(1)} %pad_maximum_fusion.79), channel_id=1, replica_groups=mesh['span'=16,'flow'=32] {'span','flow'}, use_global_device_ids=true, to_apply=%region_26.27 | all-reduce | flops 3 | bytes 24 | tf_op jit(solution)/shard_map/psum | solution.py:105
  1009.9 94.4 %psum.142 = f32[]{:T(128)} all-reduce(f32[]{:T(128)S(6)} %add.499), channel_id=1, replica_groups=mesh['span'=16,'flow'=32] {'span','flow'}, use_global_device_ids=true, to_apply=%region_29.30 | all-reduce | flops 1 | bytes 8 | tf_op jit(solution)/shard_map/psum | solution.py:110
  1123.3 104.2 %psum.143 = f32[32,128]{1,0:T(8,128)S(1)} all-reduce(f32[32,128]{1,0:T(8,128)S(1)} %broadcast_multiply_fusion.2), channel_id=1, replica_groups=mesh['span'=16,'flow'=32] {'flow'}, use_global_device_ids=true, to_apply=%region_31.32 | all-reduce | flops 4096 | bytes 32768 | tf_op jit(solution)/shard_map/psum | solution.py:97
  1227.5 6.3 collective-permute-start.21
  1242.7 97.3 %psum.144 = f32[4]{0:T(128)S(1)} all-reduce(f32[4]{0:T(128)S(1)} %pad_maximum_fusion.80), channel_id=1, replica_groups=mesh['span'=16,'flow'=32] {'span','flow'}, use_global_device_ids=true, to_apply=%region_39.40 | all-reduce | flops 4 | bytes 32 | tf_op jit(solution)/shard_map/psum | solution.py:105
  1348.2 94.6 %psum.145 = f32[]{:T(128)} all-reduce(f32[]{:T(128)S(6)} %add.518), channel_id=1, replica_groups=mesh['span'=16,'flow'=32] {'span','flow'}, use_global_device_ids=true, to_apply=%region_42.43 | all-reduce | flops 1 | bytes 8 | tf_op jit(solution)/shard_map/psum | solution.py:110
  1462.9 104.2 %psum.146 = f32[32,128]{1,0:T(8,128)S(1)} all-reduce(f32[32,128]{1,0:T(8,128)S(1)} %broadcast_multiply_fusion.1), channel_id=1, replica_groups=mesh['span'=16,'flow'=32] {'flow'}, use_global_device_ids=true, to_apply=%region_44.45 | all-reduce | flops 4096 | bytes 32768 | tf_op jit(solution)/shard_map/psum | solution.py:97
  1567.2 6.3 collective-permute-start.27
  1583.6 97.3 %psum.147 = f32[5]{0:T(128)S(1)} all-reduce(f32[5]{0:T(128)S(1)} %stack.96), channel_id=1, replica_groups=mesh['span'=16,'flow'=32] {'span','flow'}, use_global_device_ids=true, to_apply=%region_54.55 | all-reduce | flops 5 | bytes 40 | tf_op jit(solution)/shard_map/psum | solution.py:105
  1690.2 94.5 %psum.148 = f32[]{:T(128)} all-reduce(f32[]{:T(128)S(6)} %add.539), channel_id=1, replica_groups=mesh['span'=16,'flow'=32] {'span','flow'}, use_global_device_ids=true, to_apply=%region_57.58 | all-reduce | flops 1 | bytes 8 | tf_op jit(solution)/shard_map/psum | solution.py:110
  1806.0 104.2 %psum.149 = f32[32,128]{1,0:T(8,128)S(1)} all-reduce(f32[32,128]{1,0:T(8,128)S(1)} %broadcast_multiply_fusion), channel_id=1, replica_groups=mesh['span'=16,'flow'=32] {'flow'}, use_global_device_ids=true, to_apply=%region_59.60 | all-reduce | flops 4096 | bytes 32768 | tf_op jit(solution)/shard_map/psum | solution.py:97
  1928.0 97.2 %psum.150 = f32[6]{0:T(128)S(1)} all-reduce(f32[6]{0:T(128)S(1)} %stack.103), channel_id=1, replica_groups=mesh['span'=16,'flow'=32] {'span','flow'}, use_global_device_ids=true, to_apply=%region_71.72 | all-reduce | flops 6 | bytes 48 | tf_op jit(solution)/shard_map/psum | solution.py:105
  2043.5 94.5 %psum.151 = f32[]{:T(128)} all-reduce(f32[]{:T(128)S(6)} %add.562), channel_id=1, replica_groups=mesh['span'=16,'flow'=32] {'span','flow'}, use_global_device_ids=true, to_apply=%region_74.75 | all-reduce | flops 1 | bytes 8 | tf_op jit(solution)/shard_map/psum | solution.py:110
  (214 shorter events, 158.0 us)
Async XLA Ops:
  111.6 118.8 %collective-permute-start.1 = (f32[6,1,8,128]{3,2,1,0:T(8,128)S(1)}, f32[6,1,8,128]{3,2,1,0:T(8,128)S(1)}, u32[]{:S(2)}, u32[]{:S(2)}) collective-permute-start(f32[6,1,8,128]{3,2,1,0:T(8,128)S(1)} %get-tuple-element.192), channel_id=1, source_target_pairs={{32,0},{64,32},{96,64},{128,96},{160,128},{192,160},{224,192},{256... | collective-permute-start | bytes 73736 | tf_op jit(solution)/shard_map/ppermute | solution.py:17
  112.9 117.5 %collective-permute-start = (f32[6,1,8,128]{3,2,1,0:T(8,128)S(1)}, f32[6,1,8,128]{3,2,1,0:T(8,128)S(1)}, u32[]{:S(2)}, u32[]{:S(2)}) collective-permute-start(f32[6,1,8,128]{3,2,1,0:T(8,128)S(1)} %get-tuple-element.191), channel_id=1, source_target_pairs={{0,32},{32,64},{64,96},{96,128},{128,160},{160,192},{192,224},{224... | collective-permute-start | bytes 73736 | tf_op jit(solution)/shard_map/ppermute | solution.py:16
  118.4 120.2 %collective-permute-start.5 = (f32[1,128]{1,0:T(1,128)S(1)}, f32[1,128]{1,0:T(1,128)S(1)}, u32[]{:S(2)}, u32[]{:S(2)}) collective-permute-start(f32[1,128]{1,0:T(1,128)S(1)} %get-tuple-element.224), channel_id=1, source_target_pairs={{32,0},{64,32},{96,64},{128,96},{160,128},{192,160},{224,192},{256... | collective-permute-start | bytes 1544 | tf_op jit(solution)/shard_map/ppermute | solution.py:17
  119.7 119.0 %collective-permute-start.4 = (f32[1,128]{1,0:T(1,128)S(1)}, f32[1,128]{1,0:T(1,128)S(1)}, u32[]{:S(2)}, u32[]{:S(2)}) collective-permute-start(f32[1,128]{1,0:T(1,128)S(1)} %get-tuple-element.223), channel_id=1, source_target_pairs={{0,32},{32,64},{64,96},{96,128},{128,160},{160,192},{192,224},{224... | collective-permute-start | bytes 1544 | tf_op jit(solution)/shard_map/ppermute | solution.py:16
  439.9 120.0 %collective-permute-start.7 = (f32[6,1,8,128]{3,2,1,0:T(8,128)S(1)}, f32[6,1,8,128]{3,2,1,0:T(8,128)S(1)}, u32[]{:S(2)}, u32[]{:S(2)}) collective-permute-start(f32[6,1,8,128]{3,2,1,0:T(8,128)S(1)} %get-tuple-element.180), channel_id=1, source_target_pairs={{32,0},{64,32},{96,64},{128,96},{160,128},{192,160},{224,192},{256... | collective-permute-start | bytes 73736 | tf_op jit(solution)/shard_map/ppermute | solution.py:17
  441.2 118.7 %collective-permute-start.6 = (f32[6,1,8,128]{3,2,1,0:T(8,128)S(1)}, f32[6,1,8,128]{3,2,1,0:T(8,128)S(1)}, u32[]{:S(2)}, u32[]{:S(2)}) collective-permute-start(f32[6,1,8,128]{3,2,1,0:T(8,128)S(1)} %get-tuple-element.179), channel_id=1, source_target_pairs={{0,32},{32,64},{64,96},{96,128},{128,160},{160,192},{192,224},{224... | collective-permute-start | bytes 73736 | tf_op jit(solution)/shard_map/ppermute | solution.py:16
  449.2 119.0 %collective-permute-start.11 = (f32[1,128]{1,0:T(1,128)S(1)}, f32[1,128]{1,0:T(1,128)S(1)}, u32[]{:S(2)}, u32[]{:S(2)}) collective-permute-start(f32[1,128]{1,0:T(1,128)S(1)} %get-tuple-element.218), channel_id=1, source_target_pairs={{32,0},{64,32},{96,64},{128,96},{160,128},{192,160},{224,192},{256... | collective-permute-start | bytes 1544 | tf_op jit(solution)/shard_map/ppermute | solution.py:17
  450.5 117.7 %collective-permute-start.10 = (f32[1,128]{1,0:T(1,128)S(1)}, f32[1,128]{1,0:T(1,128)S(1)}, u32[]{:S(2)}, u32[]{:S(2)}) collective-permute-start(f32[1,128]{1,0:T(1,128)S(1)} %get-tuple-element.217), channel_id=1, source_target_pairs={{0,32},{32,64},{64,96},{96,128},{128,160},{160,192},{192,224},{224... | collective-permute-start | bytes 1544 | tf_op jit(solution)/shard_map/ppermute | solution.py:16
  771.0 120.8 %collective-permute-start.13 = (f32[6,1,8,128]{3,2,1,0:T(8,128)S(1)}, f32[6,1,8,128]{3,2,1,0:T(8,128)S(1)}, u32[]{:S(2)}, u32[]{:S(2)}) collective-permute-start(f32[6,1,8,128]{3,2,1,0:T(8,128)S(1)} %get-tuple-element.174), channel_id=1, source_target_pairs={{32,0},{64,32},{96,64},{128,96},{160,128},{192,160},{224,192},{256... | collective-permute-start | bytes 73736 | tf_op jit(solution)/shard_map/ppermute | solution.py:17
  772.3 119.6 %collective-permute-start.12 = (f32[6,1,8,128]{3,2,1,0:T(8,128)S(1)}, f32[6,1,8,128]{3,2,1,0:T(8,128)S(1)}, u32[]{:S(2)}, u32[]{:S(2)}) collective-permute-start(f32[6,1,8,128]{3,2,1,0:T(8,128)S(1)} %get-tuple-element.173), channel_id=1, source_target_pairs={{0,32},{32,64},{64,96},{96,128},{128,160},{160,192},{192,224},{224... | collective-permute-start | bytes 73736 | tf_op jit(solution)/shard_map/ppermute | solution.py:16
  780.8 119.4 %collective-permute-start.17 = (f32[1,128]{1,0:T(1,128)S(1)}, f32[1,128]{1,0:T(1,128)S(1)}, u32[]{:S(2)}, u32[]{:S(2)}) collective-permute-start(f32[1,128]{1,0:T(1,128)S(1)} %get-tuple-element.212), channel_id=1, source_target_pairs={{32,0},{64,32},{96,64},{128,96},{160,128},{192,160},{224,192},{256... | collective-permute-start | bytes 1544 | tf_op jit(solution)/shard_map/ppermute | solution.py:17
  782.1 118.1 %collective-permute-start.16 = (f32[1,128]{1,0:T(1,128)S(1)}, f32[1,128]{1,0:T(1,128)S(1)}, u32[]{:S(2)}, u32[]{:S(2)}) collective-permute-start(f32[1,128]{1,0:T(1,128)S(1)} %get-tuple-element.211), channel_id=1, source_target_pairs={{0,32},{32,64},{64,96},{96,128},{128,160},{160,192},{192,224},{224... | collective-permute-start | bytes 1544 | tf_op jit(solution)/shard_map/ppermute | solution.py:16
  1105.4 122.1 %collective-permute-start.19 = (f32[6,1,8,128]{3,2,1,0:T(8,128)S(1)}, f32[6,1,8,128]{3,2,1,0:T(8,128)S(1)}, u32[]{:S(2)}, u32[]{:S(2)}) collective-permute-start(f32[6,1,8,128]{3,2,1,0:T(8,128)S(1)} %get-tuple-element.168), channel_id=1, source_target_pairs={{32,0},{64,32},{96,64},{128,96},{160,128},{192,160},{224,192},{256... | collective-permute-start | bytes 73736 | tf_op jit(solution)/shard_map/ppermute | solution.py:17
  1106.7 120.8 %collective-permute-start.18 = (f32[6,1,8,128]{3,2,1,0:T(8,128)S(1)}, f32[6,1,8,128]{3,2,1,0:T(8,128)S(1)}, u32[]{:S(2)}, u32[]{:S(2)}) collective-permute-start(f32[6,1,8,128]{3,2,1,0:T(8,128)S(1)} %get-tuple-element.167), channel_id=1, source_target_pairs={{0,32},{32,64},{64,96},{96,128},{128,160},{160,192},{192,224},{224... | collective-permute-start | bytes 73736 | tf_op jit(solution)/shard_map/ppermute | solution.py:16
  1116.5 119.4 %collective-permute-start.23 = (f32[1,128]{1,0:T(1,128)S(1)}, f32[1,128]{1,0:T(1,128)S(1)}, u32[]{:S(2)}, u32[]{:S(2)}) collective-permute-start(f32[1,128]{1,0:T(1,128)S(1)} %get-tuple-element.206), channel_id=1, source_target_pairs={{32,0},{64,32},{96,64},{128,96},{160,128},{192,160},{224,192},{256... | collective-permute-start | bytes 1544 | tf_op jit(solution)/shard_map/ppermute | solution.py:17
  1117.8 118.1 %collective-permute-start.22 = (f32[1,128]{1,0:T(1,128)S(1)}, f32[1,128]{1,0:T(1,128)S(1)}, u32[]{:S(2)}, u32[]{:S(2)}) collective-permute-start(f32[1,128]{1,0:T(1,128)S(1)} %get-tuple-element.205), channel_id=1, source_target_pairs={{0,32},{32,64},{64,96},{96,128},{128,160},{160,192},{192,224},{224... | collective-permute-start | bytes 1544 | tf_op jit(solution)/shard_map/ppermute | solution.py:16
  1443.8 123.4 %collective-permute-start.25 = (f32[6,1,8,128]{3,2,1,0:T(8,128)S(1)}, f32[6,1,8,128]{3,2,1,0:T(8,128)S(1)}, u32[]{:S(2)}, u32[]{:S(2)}) collective-permute-start(f32[6,1,8,128]{3,2,1,0:T(8,128)S(1)} %get-tuple-element.162), channel_id=1, source_target_pairs={{32,0},{64,32},{96,64},{128,96},{160,128},{192,160},{224,192},{256... | collective-permute-start | bytes 73736 | tf_op jit(solution)/shard_map/ppermute | solution.py:17
  1445.1 122.1 %collective-permute-start.24 = (f32[6,1,8,128]{3,2,1,0:T(8,128)S(1)}, f32[6,1,8,128]{3,2,1,0:T(8,128)S(1)}, u32[]{:S(2)}, u32[]{:S(2)}) collective-permute-start(f32[6,1,8,128]{3,2,1,0:T(8,128)S(1)} %get-tuple-element.161), channel_id=1, source_target_pairs={{0,32},{32,64},{64,96},{96,128},{128,160},{160,192},{192,224},{224... | collective-permute-start | bytes 73736 | tf_op jit(solution)/shard_map/ppermute | solution.py:16
  1456.1 119.4 %collective-permute-start.29 = (f32[1,128]{1,0:T(1,128)S(1)}, f32[1,128]{1,0:T(1,128)S(1)}, u32[]{:S(2)}, u32[]{:S(2)}) collective-permute-start(f32[1,128]{1,0:T(1,128)S(1)} %get-tuple-element.200), channel_id=1, source_target_pairs={{32,0},{64,32},{96,64},{128,96},{160,128},{192,160},{224,192},{256... | collective-permute-start | bytes 1544 | tf_op jit(solution)/shard_map/ppermute | solution.py:17
  1457.4 118.1 %collective-permute-start.28 = (f32[1,128]{1,0:T(1,128)S(1)}, f32[1,128]{1,0:T(1,128)S(1)}, u32[]{:S(2)}, u32[]{:S(2)}) collective-permute-start(f32[1,128]{1,0:T(1,128)S(1)} %get-tuple-element.199), channel_id=1, source_target_pairs={{0,32},{32,64},{64,96},{96,128},{128,160},{160,192},{192,224},{224... | collective-permute-start | bytes 1544 | tf_op jit(solution)/shard_map/ppermute | solution.py:16
  1785.7 124.6 %collective-permute-start.31 = (f32[6,1,8,128]{3,2,1,0:T(8,128)S(1)}, f32[6,1,8,128]{3,2,1,0:T(8,128)S(1)}, u32[]{:S(2)}, u32[]{:S(2)}) collective-permute-start(f32[6,1,8,128]{3,2,1,0:T(8,128)S(1)} %get-tuple-element.156), channel_id=1, source_target_pairs={{32,0},{64,32},{96,64},{128,96},{160,128},{192,160},{224,192},{256... | collective-permute-start | bytes 73736 | tf_op jit(solution)/shard_map/ppermute | solution.py:17
  1787.0 123.3 %collective-permute-start.30 = (f32[6,1,8,128]{3,2,1,0:T(8,128)S(1)}, f32[6,1,8,128]{3,2,1,0:T(8,128)S(1)}, u32[]{:S(2)}, u32[]{:S(2)}) collective-permute-start(f32[6,1,8,128]{3,2,1,0:T(8,128)S(1)} %get-tuple-element.155), channel_id=1, source_target_pairs={{0,32},{32,64},{64,96},{96,128},{128,160},{160,192},{192,224},{224... | collective-permute-start | bytes 73736 | tf_op jit(solution)/shard_map/ppermute | solution.py:16
  1799.2 119.3 %collective-permute-start.35 = (f32[1,128]{1,0:T(1,128)S(1)}, f32[1,128]{1,0:T(1,128)S(1)}, u32[]{:S(2)}, u32[]{:S(2)}) collective-permute-start(f32[1,128]{1,0:T(1,128)S(1)} %get-tuple-element.194), channel_id=1, source_target_pairs={{32,0},{64,32},{96,64},{128,96},{160,128},{192,160},{224,192},{256... | collective-permute-start | bytes 1544 | tf_op jit(solution)/shard_map/ppermute | solution.py:17
  1800.5 118.0 %collective-permute-start.34 = (f32[1,128]{1,0:T(1,128)S(1)}, f32[1,128]{1,0:T(1,128)S(1)}, u32[]{:S(2)}, u32[]{:S(2)}) collective-permute-start(f32[1,128]{1,0:T(1,128)S(1)} %get-tuple-element.193), channel_id=1, source_target_pairs={{0,32},{32,64},{64,96},{96,128},{128,160},{160,192},{192,224},{224... | collective-permute-start | bytes 1544 | tf_op jit(solution)/shard_map/ppermute | solution.py:16
  (18 other events, 228.2 us)
where the time goes:
time: 2150 us; the launch traced here: 2140 us
  blocking collectives  1880 us (87%)
  starting transfers between devices  131 us (6%)
  between operations  71.4 us (3%)
  other arithmetic  50.6 us (2%)
    psum x6, blocking collectives, shards(): sink = lax.psum(jnp.dot(metal_pick, wall_vals, precision=highest), 'flow')  623 us
    psum x6, blocking collectives, shards(): values = lax.psum(terms, ('span', 'flow'))  583 us
    psum x6, blocking collectives, shards(): lax.psum(local_inner((image_f, image_s), (image_f, image_s)), ('span', 'f...  568 us
    psum x1, blocking collectives, shards(): lax.psum(local_inner((rhs_fluid, rhs_solid), (rhs_fluid, rhs_solid)), ('s...  106 us
    ppermute x18, starting transfers between devices, extended(): before = lax.ppermute(last, axis, up)  77.4 us
    ppermute x18, starting transfers between devices, extended(): after = lax.ppermute(first, axis, down)  53.6 us
  transfers between devices with their start and end apart: 36, of which 0 were waited for; matrix products, arithmetic and copies ran while one was open for 0% of the time, Pallas kernels for 0%

commit v1 on v0

--- a/solution.py
+++ b/solution.py
@@ -1,9 +1,15 @@
+import functools
+
 import jax
 import jax.numpy as jnp
 from jax import lax
+from jax.experimental import pallas as pl
+from jax.experimental.pallas import tpu as pltpu
 from jax.sharding import PartitionSpec as P
 
 KRYLOV = 6
+MESH = pl.DeviceIdType.MESH
+EARLY = 4
 
 
 def extended(shard, sides, width):
@@ -19,9 +25,19 @@
     return shard
 
 
-def least_squares(hess, beta, steps):
+def back_substitute(upper, rhs_g, steps):
+    coeffs = [None] * steps
+    for j in range(steps - 1, -1, -1):
+        total = rhs_g[j]
+        for k in range(j + 1, steps):
+            total = total - upper[k][j] * coeffs[k]
+        coeffs[j] = total / upper[j][j]
+    return coeffs
+
+
+def least_squares(hess, beta, zero, steps):
     cos_list, sin_list, upper = ([], [], [])
-    rhs_g = [beta] + [jnp.float32(0.0) for _ in range(steps)]
+    rhs_g = [beta] + [zero for _ in range(steps)]
     for j in range(steps):
         column = [hess[i][j] for i in range(j + 2)]
         for i in range(j):
@@ -37,16 +53,10 @@
         cos_list.append(cos_now)
         sin_list.append(sin_now)
         upper.append(column[: j + 1])
-    coeffs = [None] * steps
-    for j in range(steps - 1, -1, -1):
-        total = rhs_g[j]
-        for k in range(j + 1, steps):
-            total = total - upper[k][j] * coeffs[k]
-        coeffs[j] = total / upper[j][j]
-    return coeffs
-
-
-def shards(rhs_fluid, rhs_solid, blocks, weights, kdiag, wall_fluid, wall_solid, wall_coef):
+    return back_substitute(upper, rhs_g, steps)
+
+
+def arnoldi(rhs_fluid, rhs_solid, blocks, weights, kdiag, wall_fluid, wall_solid, wall_coef):
     rows_a = rhs_fluid.shape[1]
     rows_b = rhs_fluid.shape[2]
     width = rhs_fluid.shape[3]
@@ -100,7 +110,6 @@
             upad[:-2] + upad[2:] + jnp.roll(metal_u, 1, axis=1) + jnp.roll(metal_u, -1, axis=1)
         )
         image_s = (4.0 + kdiag) * metal_u - beside_all - sink
-        image_f, image_s = (image_f, image_s)
         terms = jnp.stack([local_inner(basis[i], (image_f, image_s)) for i in range(j + 1)])
         values = lax.psum(terms, ("span", "flow"))
         for i in range(j + 1):
@@ -113,13 +122,472 @@
             hess[i][j] = values[i]
         hess[j + 1][j] = rest
         basis.append((image_f / rest, image_s / rest))
-    coeffs = least_squares(hess, beta, KRYLOV)
+    coeffs = least_squares(hess, beta, jnp.float32(0.0), KRYLOV)
     x_fluid = jnp.zeros_like(rhs_fluid)
     x_solid = jnp.zeros_like(rhs_solid)
     for j in range(KRYLOV):
         x_fluid = x_fluid + coeffs[j] * basis[j][0]
         x_solid = x_solid + coeffs[j] * basis[j][1]
     return (x_fluid, x_solid)
+
+
+def kernel(
+    ns, nf,
+    rf_hbm, rs_hbm, bl_hbm, we_hbm, kd_hbm, wf_ref, ws_ref, wc_ref,
+    xf_ref, xs_ref, ok_ref,
+    z, u, q, bl, we, wm, kd, hs, hq, sq, he, wall, place, pairs, scal, ra, rb,
+    in_sem, s_halo, r_halo, s_edge, r_edge, s_wall, r_wall, s_red, r_red,
+):
+    f32 = jnp.float32
+    s = lax.axis_index("span")
+    f = lax.axis_index("flow")
+    up = (lax.rem(s + 1, ns), f)
+    down = (lax.rem(s + ns - 1, ns), f)
+    right = (s, lax.rem(f + 1, nf))
+    left = (s, lax.rem(f + nf - 1, nf))
+
+    loads = [
+        pltpu.make_async_copy(rf_hbm, z.at[0], in_sem.at[0]),
+        pltpu.make_async_copy(rs_hbm, u.at[0], in_sem.at[1]),
+        pltpu.make_async_copy(we_hbm, we, in_sem.at[2]),
+        pltpu.make_async_copy(bl_hbm, bl, in_sem.at[3]),
+        pltpu.make_async_copy(kd_hbm, kd, in_sem.at[4]),
+    ]
+    for load in loads:
+        load.start()
+
+    barrier = pltpu.get_barrier_semaphore()
+
+    def greet_flow(d, c):
+        pl.semaphore_signal(barrier, inc=1, device_id=(s, lax.rem(f + d, nf)), device_id_type=MESH)
+        return c
+
+    def greet_span(d, c):
+        pl.semaphore_signal(barrier, inc=1, device_id=(lax.rem(s + d, ns), f), device_id_type=MESH)
+        return c
+
+    lax.fori_loop(1, ns, greet_span, 0)
+    lax.fori_loop(1, nf, greet_flow, 0)
+
+    row8 = lax.broadcasted_iota(jnp.int32, (8, 128), 0)
+    row16 = lax.broadcasted_iota(jnp.int32, (2, 8, 128), 0) * 8 + lax.broadcasted_iota(
+        jnp.int32, (2, 8, 128), 1
+    )
+    row32 = lax.broadcasted_iota(jnp.int32, (32, 128), 0)
+    lane32 = lax.broadcasted_iota(jnp.int32, (32, 128), 1)
+    eye = row32 == lane32
+    patch = wf_ref[0, 0]
+    metal_row = ws_ref[0, 0]
+    coef = wc_ref[0]
+    wall_mask = jnp.where(row16 == patch, 1.0, 0.0).astype(f32)
+    metal_mask = jnp.where(row32 == metal_row, 1.0, 0.0).astype(f32)
+    lane1 = lax.broadcasted_iota(jnp.int32, (1, 128), 1)
+    place[pl.ds(f, 1), :] = jnp.where(lane1 == f, metal_row.astype(f32), 0.0)
+    has_down = jnp.where(s > 0, 1.0, 0.0).astype(f32)
+    has_up = jnp.where(s < ns - 1, 1.0, 0.0).astype(f32)
+    has_left = jnp.where(f > 0, 1.0, 0.0).astype(f32)
+    has_right = jnp.where(f < nf - 1, 1.0, 0.0).astype(f32)
+
+    def send_rows_flow(buf, k):
+        def one(d, c):
+            pltpu.make_async_remote_copy(
+                src_ref=buf.at[pl.ds(f, 1)], dst_ref=buf.at[pl.ds(f, 1)],
+                send_sem=s_wall.at[k], recv_sem=r_wall.at[k],
+                device_id=(s, lax.rem(f + d, nf)), device_id_type=MESH,
+            ).start()
+            return c
+
+        lax.fori_loop(1, nf, one, 0)
+
+    def rows_flow(buf, k):
+        return pltpu.make_async_remote_copy(
+            src_ref=buf.at[pl.ds(0, nf - 1)], dst_ref=buf.at[pl.ds(0, nf - 1)],
+            send_sem=s_wall.at[k], recv_sem=r_wall.at[k], device_id=right, device_id_type=MESH,
+        )
+
+    def send_rows_span(buf, k):
+        def one(d, c):
+            pltpu.make_async_remote_copy(
+                src_ref=buf.at[pl.ds(s, 1)], dst_ref=buf.at[pl.ds(s, 1)],
+                send_sem=s_red.at[k], recv_sem=r_red.at[k],
+                device_id=(lax.rem(s + d, ns), f), device_id_type=MESH,
+            ).start()
+            return c
+
+        lax.fori_loop(1, ns, one, 0)
+
+    def rows_span(buf, k):
+        return pltpu.make_async_remote_copy(
+            src_ref=buf.at[pl.ds(0, ns - 1)], dst_ref=buf.at[pl.ds(0, ns - 1)],
+            send_sem=s_red.at[k], recv_sem=r_red.at[k], device_id=up, device_id_type=MESH,
+        )
+
+    def halos(k):
+        def copy(n, src, dst, to):
+            return pltpu.make_async_remote_copy(
+                src_ref=src, dst_ref=dst, send_sem=s_halo.at[k, n], recv_sem=r_halo.at[k, n],
+                device_id=to, device_id_type=MESH,
+            )
+
+        return [
+            copy(0, z.at[k, :, 1], hs.at[k, 0], up),
+            copy(1, z.at[k, :, 0], hs.at[k, 1], down),
+            copy(2, sq.at[k, 0], hq.at[k, 0], right),
+            copy(3, sq.at[k, 1], hq.at[k, 1], left),
+        ]
+
+    def edges(k):
+        def copy(n, src, dst, to):
+            return pltpu.make_async_remote_copy(
+                src_ref=src, dst_ref=dst, send_sem=s_edge.at[k, n], recv_sem=r_edge.at[k, n],
+                device_id=to, device_id_type=MESH,
+            )
+
+        return [
+            copy(0, u.at[k, pl.ds(31, 1)], he.at[k, 0, pl.ds(0, 1)], up),
+            copy(1, u.at[k, pl.ds(0, 1)], he.at[k, 1, pl.ds(0, 1)], down),
+        ]
+
+    def send_halos(k):
+        out = halos(k)
+        out[0].start()
+        out[1].start()
+        for g in range(6):
+            for a in range(2):
+                i = 2 * g + a
+                sq[k, 0, i : i + 1, :] = z[k, g, a, 7:8, :]
+                sq[k, 1, i : i + 1, :] = z[k, g, a, 0:1, :]
+        out[2].start()
+        out[3].start()
+
+    def local_part(k):
+        field = [z[k, g] for g in range(6)]
+        for g in range(6):
+            v = field[g]
+            total = bl[g, 0] * field[0]
+            for h in range(1, 6):
+                total = total + bl[g, h] * field[h]
+            total = total - we[4] * pltpu.roll(v, 1, 2) - we[5] * pltpu.roll(v, 127, 2)
+            total = total - wm[0] * pltpu.roll(v, 1, 1) - wm[1] * pltpu.roll(v, 7, 1)
+            z[k + 1, g, 0] = total[0] - we[1, 0] * v[1]
+            z[k + 1, g, 1] = total[1] - we[0, 1] * v[0]
+
+    def halo_part(k, metal_here):
+        inflow = coef * metal_here
+        for g in range(6):
+            for a in range(2):
+                i = 2 * g + a
+                total = z[k + 1, g, a]
+                if a == 0:
+                    total = total - wm[4, 0] * hs[k, 0, g]
+                else:
+                    total = total - wm[4, 1] * hs[k, 1, g]
+                total = total - wm[2, a] * hq[k, 0, i : i + 1, :] - wm[3, a] * hq[k, 1, i : i + 1, :]
+                if g == 5:
+                    total = total - wall_mask[a] * inflow
+                z[k + 1, g, a] = total
+
+    def own_metal(values):
+        return jnp.sum(metal_mask * values, axis=0, keepdims=True)
+
+    def wall_value(k):
+        picked = wall_mask[0] * z[k, 5, 0] + wall_mask[1] * z[k, 5, 1]
+        return coef * jnp.sum(picked, axis=0, keepdims=True)
+
+    def metal_local(k):
+        v = u[k]
+        total = (4.0 + kd[...]) * v - pltpu.roll(v, 1, 1) - pltpu.roll(v, 127, 1)
+        below = jnp.where(row32 == 0, has_down * he[k, 0, 0:1, :], pltpu.roll(v, 1, 0))
+        above = jnp.where(row32 == 31, has_up * he[k, 1, 0:1, :], pltpu.roll(v, 31, 0))
+        return total - below - above
+
+    def dot_row(store, i, j, own_i, own_j):
+        total = store[i, 0, 0] * store[j, 0, 0] + store[i, 0, 1] * store[j, 0, 1]
+        for g in range(1, 6):
+            total = total + store[i, g, 0] * store[j, g, 0] + store[i, g, 1] * store[j, g, 1]
+        return jnp.sum(total, axis=0, keepdims=True) + own_i * own_j
+
+    def packed():
+        sums = jnp.sum(pairs[...], axis=1, keepdims=True)
+        return jnp.sum(jnp.where(eye, sums, 0.0), axis=0, keepdims=True)
+
+    def unpack(total):
+        sums = jnp.sum(jnp.where(eye, total, 0.0), axis=1, keepdims=True)
+        scal[...] = jnp.broadcast_to(sums, (32, 128))
+
+    loads[0].wait()
+    for g in range(6):
+        for a in range(2):
+            i = 2 * g + a
+            sq[0, 0, i : i + 1, :] = z[0, g, a, 7:8, :]
+            sq[0, 1, i : i + 1, :] = z[0, g, a, 0:1, :]
+    sq[:, :, 12:16, :] = jnp.zeros((KRYLOV, 2, 4, 128), f32)
+    pl.semaphore_wait(barrier, ns + nf - 2)
+    for copy in halos(0):
+        copy.start()
+    loads[1].wait()
+    for copy in edges(0):
+        copy.start()
+    pairs[...] = jnp.zeros((32, 128), f32)
+    loads[2].wait()
+    wm[0] = jnp.where(row8 == 0, 0.0, we[2])
+    wm[1] = jnp.where(row8 == 7, 0.0, we[3])
+    wm[2] = jnp.where(row8 == 0, has_left * we[2], 0.0)
+    wm[3] = jnp.where(row8 == 7, has_right * we[3], 0.0)
+    wm[4, 0] = has_down * we[0, 0]
+    wm[4, 1] = has_up * we[1, 1]
+    loads[3].wait()
+    loads[4].wait()
+
+    own = []
+    walls = []
+    pick = None
+    coef_a = coef_b = None
+    for k in range(KRYLOV):
+        if k > 0:
+            send_halos(k)
+        mine = wall_value(k)
+        walls.append(mine)
+        if k < KRYLOV - 1:
+            wall[k, pl.ds(f, 1), :] = mine
+            send_rows_flow(wall.at[k], k)
+        if k == 0:
+            send_rows_flow(place, KRYLOV - 1)
+        local_part(k)
+        if k > 0:
+            if k == 1:
+                rows_flow(place, KRYLOV - 1).wait_recv()
+                places = jnp.sum(place[...], axis=0, keepdims=True)
+                pick = jnp.where((row32.astype(f32) == places) & (lane32 < 32), 1.0, 0.0)[:, 0:32]
+            rows_flow(wall.at[k - 1], k - 1).wait_recv()
+            sink = jnp.dot(
+                pick, wall[k - 1], precision=lax.Precision.HIGHEST, preferred_element_type=f32
+            )
+            for copy in edges(k - 1):
+                copy.wait_recv()
+            u[k] = metal_local(k - 1) - sink
+            for copy in edges(k):
+                copy.start()
+        own.append(own_metal(u[k]))
+        if k == EARLY - 1:
+            n = 0
+            for i in range(EARLY):
+                for j in range(i, EARLY):
+                    pairs[n : n + 1, :] = dot_row(z, i, j, own[i], own[j])
+                    n += 1
+            ra[0, pl.ds(f, 1), :] = packed()
+            send_rows_flow(ra.at[0], KRYLOV)
+        if k == EARLY:
+            rows_flow(ra.at[0], KRYLOV).wait_recv()
+            rb[0, pl.ds(s, 1), :] = jnp.sum(ra[0], axis=0, keepdims=True)
+            send_rows_span(rb.at[0], 0)
+        if k == EARLY + 1:
+            rows_span(rb.at[0], 0).wait_recv()
+            unpack(jnp.sum(rb[0], axis=0, keepdims=True))
+            gram = {}
+            n = 0
+            for i in range(EARLY):
+                for j in range(i, EARLY):
+                    gram[i, j] = scal[n : n + 1, :]
+                    n += 1
+            r = {}
+            inv = []
+            trust = []
+            for i in range(EARLY):
+                for j in range(i, EARLY):
+                    t = gram[i, j]
+                    for h in range(i):
+                        t = t - r[h, i] * r[h, j]
+                    if i == j:
+                        floor = gram[i, i] * 1e-5
+                        trust.append(t > floor)
+                        t = jnp.maximum(t, floor)
+                        inv.append(lax.rsqrt(t))
+                    r[i, j] = t * inv[i]
+            ratio = [r[i, i + 1] * inv[i] for i in range(EARLY - 1)]
+            coef_a = [ratio[0]]
+            coef_b = [None, r[1, 1] * inv[0]]
+            good = trust[1]
+            for i in range(1, EARLY - 1):
+                good = good & trust[i + 1]
+                coef_a.append(jnp.where(good, ratio[i] - ratio[i - 1], coef_a[i - 1]))
+                guess = coef_b[1] * 1.22
+                coef_b.append(jnp.where(good, r[i + 1, i + 1] * inv[i], guess))
+            while len(coef_a) < KRYLOV:
+                coef_a.append(coef_a[-1])
+            while len(coef_b) < KRYLOV + 1:
+                coef_b.append(coef_b[-1])
+            poly = [[inv[0]]]
+            for i in range(KRYLOV):
+                back = 1.0 / coef_b[i + 1]
+                new = []
+                for j in range(i + 2):
+                    t = None
+                    if j >= 1:
+                        t = poly[i][j - 1]
+                    if j <= i:
+                        t = -coef_a[i] * poly[i][j] if t is None else t - coef_a[i] * poly[i][j]
+                    if i >= 1 and j <= i - 1:
+                        t = t - coef_b[i] * poly[i - 1][j]
+                    new.append(t * back)
+                poly.append(new)
+            size = [jnp.sqrt(gram[i, i]) for i in range(EARLY)]
+            growth = size[-1] / size[-2]
+            while len(size) < KRYLOV:
+                size.append(size[-1] * growth)
+            spread = []
+            for i in range(KRYLOV):
+                t = jnp.abs(poly[i][0]) * size[0]
+                for j in range(1, i + 1):
+                    t = t + jnp.abs(poly[i][j]) * size[j]
+                spread.append(t)
+            qown = []
+            for i in range(KRYLOV + 1):
+                for g in range(6):
+                    t = poly[i][0] * z[0, g]
+                    for j in range(1, min(i, KRYLOV - 1) + 1):
+                        t = t + poly[i][j] * z[j, g]
+                    q[i, g] = t
+                t = poly[i][0] * own[0]
+                for j in range(1, min(i, KRYLOV - 1) + 1):
+                    t = t + poly[i][j] * own[j]
+                qown.append(t)
+            n = 0
+            for i in range(KRYLOV):
+                for j in range(i + 1):
+                    pairs[n : n + 1, :] = dot_row(q, j, i, qown[j], qown[i])
+                    n += 1
+        for copy in halos(k):
+            copy.wait_recv()
+        halo_part(k, own[k])
+
+    last = KRYLOV
+    for g in range(6):
+        q[last, g] = q[last, g] + poly[last][last] * z[last, g]
+    for copy in edges(last - 1):
+        copy.wait_recv()
+    own_last = own_metal(metal_local(last - 1)) - walls[last - 1]
+    qown[last] = qown[last] + poly[last][last] * own_last
+    for j in range(last + 1):
+        n = 21 + j
+        pairs[n : n + 1, :] = dot_row(q, j, last, qown[j], qown[last])
+    ra[1, pl.ds(f, 1), :] = packed()
+    send_rows_flow(ra.at[1], KRYLOV + 1)
+    rows_flow(ra.at[1], KRYLOV + 1).wait_recv()
+    rb[1, pl.ds(s, 1), :] = jnp.sum(ra[1], axis=0, keepdims=True)
+    send_rows_span(rb.at[1], 1)
+    for k in range(KRYLOV):
+        for copy in halos(k):
+            copy.wait_send()
+        for copy in edges(k):
+            copy.wait_send()
+    for k in range(KRYLOV - 1):
+        rows_flow(wall.at[k], k).wait_send()
+    rows_flow(place, KRYLOV - 1).wait_send()
+    rows_flow(ra.at[0], KRYLOV).wait_send()
+    rows_flow(ra.at[1], KRYLOV + 1).wait_send()
+    rows_span(rb.at[0], 0).wait_send()
+    rows_span(rb.at[1], 1).wait()
+    unpack(jnp.sum(rb[1], axis=0, keepdims=True))
+    gram = {}
+    n = 0
+    for i in range(KRYLOV + 1):
+        for j in range(i + 1):
+            gram[j, i] = scal[n : n + 1, :]
+            n += 1
+    r = {}
+    low = None
+    for i in range(KRYLOV + 1):
+        scale = None
+        for j in range(i, KRYLOV + 1):
+            t = gram[i, j]
+            for h in range(i):
+                t = t - r[h, i] * r[h, j]
+            if i == j:
+                rel = t / gram[i, i]
+                low = rel if low is None else jnp.minimum(low, rel)
+                scale = lax.rsqrt(t)
+            r[i, j] = t * scale
+    zero = jnp.zeros((1, 128), f32)
+    hess = [[zero] * KRYLOV for _ in range(KRYLOV + 1)]
+    for j in range(KRYLOV):
+        for i in range(j + 2):
+            t = r[i, j + 1] * coef_b[j + 1]
+            if i <= j:
+                t = t + r[i, j] * coef_a[j]
+            if i <= j - 1:
+                t = t + r[i, j - 1] * coef_b[j]
+            hess[i][j] = t
+    y = least_squares(hess, r[0, 0] / poly[0][0], zero, KRYLOV)
+    top = jnp.abs(y[0])
+    total = jnp.abs(y[0]) * spread[0]
+    for k in range(1, KRYLOV):
+        top = jnp.maximum(top, jnp.abs(y[k]))
+        total = total + jnp.abs(y[k]) * spread[k]
+    fine = (low > 1e-2) & (total < 1e3 * top)
+    ok_ref[...] = jnp.where(fine, 1.0, 0.0)
+    for g in range(6):
+        t = y[0] * q[0, g]
+        for k in range(1, KRYLOV):
+            t = t + y[k] * q[k, g]
+        xf_ref[g] = t
+    out = None
+    for j in range(KRYLOV):
+        c = y[j] * poly[j][j]
+        for k in range(j + 1, KRYLOV):
+            c = c + y[k] * poly[k][j]
+        out = c * u[j] if out is None else out + c * u[j]
+    xs_ref[...] = out
+
+
+def shards(ns, nf, *args):
+    rhs_fluid, rhs_solid = args[0], args[1]
+    f32 = jnp.float32
+    hbm = pl.BlockSpec(memory_space=pl.ANY)
+    vmem = pl.BlockSpec(memory_space=pltpu.VMEM)
+    smem = pl.BlockSpec(memory_space=pltpu.SMEM)
+    dma = pltpu.SemaphoreType.DMA
+    x_fluid, x_solid, ok = pl.pallas_call(
+        functools.partial(kernel, ns, nf),
+        name="gmres",
+        out_shape=(
+            jax.ShapeDtypeStruct(rhs_fluid.shape, f32),
+            jax.ShapeDtypeStruct(rhs_solid.shape, f32),
+            jax.ShapeDtypeStruct((1, 128), f32),
+        ),
+        in_specs=[hbm] * 5 + [smem] * 2 + [vmem],
+        out_specs=(vmem, vmem, vmem),
+        scratch_shapes=[
+            pltpu.VMEM((KRYLOV + 1, 6, 2, 8, 128), f32),
+            pltpu.VMEM((KRYLOV, 32, 128), f32),
+            pltpu.VMEM((KRYLOV + 1, 6, 2, 8, 128), f32),
+            pltpu.VMEM((6, 6, 2, 8, 128), f32),
+            pltpu.VMEM((6, 2, 8, 128), f32),
+            pltpu.VMEM((5, 2, 8, 128), f32),
+            pltpu.VMEM((32, 128), f32),
+            pltpu.VMEM((KRYLOV, 2, 6, 8, 128), f32),
+            pltpu.VMEM((KRYLOV, 2, 16, 128), f32),
+            pltpu.VMEM((KRYLOV, 2, 16, 128), f32),
+            pltpu.VMEM((KRYLOV, 2, 8, 128), f32),
+            pltpu.VMEM((KRYLOV - 1, 32, 128), f32),
+            pltpu.VMEM((32, 128), f32),
+            pltpu.VMEM((32, 128), f32),
+            pltpu.VMEM((32, 128), f32),
+            pltpu.VMEM((2, 32, 128), f32),
+            pltpu.VMEM((2, 16, 128), f32),
+            dma((5,)),
+            dma((KRYLOV, 4)), dma((KRYLOV, 4)),
+            dma((KRYLOV, 2)), dma((KRYLOV, 2)),
+            dma((KRYLOV + 2,)), dma((KRYLOV + 2,)),
+            dma((2,)), dma((2,)),
+        ],
+        compiler_params=pltpu.CompilerParams(
+            collective_id=0, has_side_effects=True, vmem_limit_bytes=8 * 1024 * 1024
+        ),
+    )(*args)
+    return lax.cond(
+        ok[0, 0] > 0.5, lambda *a: (x_fluid, x_solid), lambda *a: arnoldi(*a), *args
+    )
 
 
 def solution(mesh):
@@ -134,4 +602,7 @@
         P("span", "flow", None),
     )
     out_specs = (P(None, "span", "flow", None), P("span", None))
-    return jax.shard_map(shards, mesh=mesh, in_specs=in_specs, out_specs=out_specs, check_vma=False)
+    return jax.shard_map(
+        functools.partial(shards, mesh.shape["span"], mesh.shape["flow"]),
+        mesh=mesh, in_specs=in_specs, out_specs=out_specs, check_vma=False,
+    )

time: 2150 us -> 60.4 us (0.03)
  blocking collectives: 1880 us -> 0 us
  starting transfers between devices: 131 us -> 0 us
  between operations: 71.4 us -> 2.1 us
  Pallas kernels: 0 us -> 56.2 us
  other arithmetic: 50.6 us -> 0 us
    psum x19 -> x0, blocking collectives: 1880 us -> none  [the longest x6 623 us: shards(): sink = lax.psum(jnp.dot(metal_pick, wall_vals, precision=highest), 'flow')]
    ppermute x36 -> x0, starting transfers between devices: 131 us -> none  [the longest x18 77.4 us: extended(): before = lax.ppermute(last, axis, up)]
    pallas_call x0 -> x1, Pallas kernels: none -> 56.2 us  [shards(): pl.pallas_call(functools.partial(kernel, ns, nf), name='gmres', out_shape...]
    reduce_sum x26 -> x0, other arithmetic: 45.7 us -> none  [the longest x13 22.9 us: local_inner(): jnp.sum(left[1] * right[1])]
  transfers between devices with their start and end apart: 36 -> 0, of which waited for: 0 -> 0; matrix products, arithmetic and copies ran while one was open for 0% -> 0% of each run, Pallas kernels for 0% -> 0%
where the time goes in v1:
time: 60.4 us; the launch traced here: 60.2 us
  Pallas kernels  56.2 us (93%)
  between operations  2.1 us (3%)
  local copies, waits for them, and re-layouts  1.85 us (3%)
    pallas_call x1, Pallas kernels, shards(): pl.pallas_call(functools.partial(kernel, ns, nf), name='gmres', out_shape...  56.2 us
    unnamed x14, local copies, waits for them, and re-layouts  1.85 us

profile of v1, /device:TPU:1, one launch (start us, length us, event | category | flops | bytes accessed | tf_op | source)
XLA Modules:
  0.0 60.2 jit_solution(9149022520660269967)
XLA Ops:
  0.6 0.0 copy-start.1
  2.0 0.0 copy-start
  2.0 0.0 copy-start.2
  2.0 0.0 copy-start.3
  2.0 0.0 copy-start.4
  2.0 56.2 %gmres.1 = (f32[6,2,8,128]{3,2,1,0:T(8,128)S(1)}, f32[32,128]{1,0:T(8,128)S(1)}, f32[1,128]{1,0:T(1,128)S(1)}) custom-call(f32[6,2,8,128]{3,2,1,0:T(8,128)} %rf_hbm.1, f32[32,128]{1,0:T(8,128)} %rs_hbm.1, f32[6,6,2,8,128]{4,3,2,1,0:T(8,128)} %bl_hbm.1, f32[6,2,8,128]{3,2,1,0:T(8,128)} %we_hbm.1, f32[32,128]{1,0:T(8,128)} %kd_hbm.1, s32[1,1]{1,0:T(1,128)S(6)} %copy.74.wf_ref, ...), custom_call_target="tpu_custom_call" | custom-call | tf_op jit(solution)/shard_map/gmres/pallas_call | solution.py:550
  58.3 0.0 copy-start.5
  58.3 0.0 copy-done.1
  58.3 0.0 copy-done
  58.3 0.0 copy-done.2
  58.3 0.0 copy-done.3
  58.3 0.0 copy-done.4
  58.3 0.6 copy-done.5
  58.9 0.6 %copy.76 = f32[6,2,8,128]{3,2,1,0:T(8,128)} copy(f32[6,2,8,128]{3,2,1,0:T(8,128)S(1)} %get-tuple-element.293) | data formatting | bytes 98304
  59.5 0.6 %copy.77 = f32[32,128]{1,0:T(8,128)} copy(f32[32,128]{1,0:T(8,128)S(1)} %get-tuple-element.294) | data formatting | bytes 32768
  (1 shorter events, 0.0 us)
Async XLA Ops:
  0.6 57.6 %copy-start.1 = (f32[6,6,2,8,128]{4,3,2,1,0:T(8,128)S(1)}, f32[6,6,2,8,128]{4,3,2,1,0:T(8,128)}, u32[]{:S(2)}) copy-start(f32[6,6,2,8,128]{4,3,2,1,0:T(8,128)} %bl_hbm.1) | copy-start | bytes 884740
  2.0 56.3 %copy-start = (f32[6,2,8,128]{3,2,1,0:T(8,128)S(1)}, f32[6,2,8,128]{3,2,1,0:T(8,128)}, u32[]{:S(2)}) copy-start(f32[6,2,8,128]{3,2,1,0:T(8,128)} %rf_hbm.1) | copy-start | bytes 147460
  2.0 56.3 %copy-start.2 = (f32[32,128]{1,0:T(8,128)S(1)}, f32[32,128]{1,0:T(8,128)}, u32[]{:S(2)}) copy-start(f32[32,128]{1,0:T(8,128)} %rs_hbm.1) | copy-start | bytes 49156
  2.0 56.3 %copy-start.3 = (f32[32,128]{1,0:T(8,128)S(1)}, f32[32,128]{1,0:T(8,128)}, u32[]{:S(2)}) copy-start(f32[32,128]{1,0:T(8,128)} %kd_hbm.1) | copy-start | bytes 49156
  2.0 56.3 %copy-start.4 = (f32[6,2,8,128]{3,2,1,0:T(8,128)S(1)}, f32[6,2,8,128]{3,2,1,0:T(8,128)}, u32[]{:S(2)}) copy-start(f32[6,2,8,128]{3,2,1,0:T(8,128)} %we_hbm.1) | copy-start | bytes 147460
  58.3 0.7 %copy-start.5 = (f32[1,1,128]{2,1,0:T(1,128)S(1)}, f32[1,1,128]{2,1,0:T(1,128)}, u32[]{:S(2)}) copy-start(f32[1,1,128]{2,1,0:T(1,128)} %wc_ref.1) | copy-start | bytes 1540

commit v2 on v1

--- a/solution.py
+++ b/solution.py
@@ -133,9 +133,9 @@
 
 def kernel(
     ns, nf,
-    rf_hbm, rs_hbm, bl_hbm, we_hbm, kd_hbm, wf_ref, ws_ref, wc_ref,
-    xf_ref, xs_ref, ok_ref,
-    z, u, q, bl, we, wm, kd, hs, hq, sq, he, wall, place, pairs, scal, ra, rb,
+    rf_hbm, rs_hbm, bl_hbm, we_hbm, kd_hbm, wf_ref, ws_ref, wc_hbm,
+    xf_ref, xs_ref, ok_ref, wc,
+    z, u, q, qm, bl, we, wm, kd, hs, hq, sq, he, wall, place, pairs, mpairs, scal, ra, rb,
     in_sem, s_halo, r_halo, s_edge, r_edge, s_wall, r_wall, s_red, r_red,
 ):
     f32 = jnp.float32
@@ -152,22 +152,29 @@
         pltpu.make_async_copy(we_hbm, we, in_sem.at[2]),
         pltpu.make_async_copy(bl_hbm, bl, in_sem.at[3]),
         pltpu.make_async_copy(kd_hbm, kd, in_sem.at[4]),
+        pltpu.make_async_copy(wc_hbm, wc, in_sem.at[5]),
     ]
     for load in loads:
         load.start()
 
     barrier = pltpu.get_barrier_semaphore()
 
-    def greet_flow(d, c):
-        pl.semaphore_signal(barrier, inc=1, device_id=(s, lax.rem(f + d, nf)), device_id_type=MESH)
+    def far_first(n, i):
+        half = lax.div(i + 1, 2)
+        return n // 2 + jnp.where(lax.rem(i, 2) == 1, half, -half)
+
+    def greet_flow(i, c):
+        to = (s, lax.rem(f + far_first(nf, i), nf))
+        pl.semaphore_signal(barrier, inc=1, device_id=to, device_id_type=MESH)
         return c
 
-    def greet_span(d, c):
-        pl.semaphore_signal(barrier, inc=1, device_id=(lax.rem(s + d, ns), f), device_id_type=MESH)
+    def greet_span(i, c):
+        to = (lax.rem(s + far_first(ns, i), ns), f)
+        pl.semaphore_signal(barrier, inc=1, device_id=to, device_id_type=MESH)
         return c
 
-    lax.fori_loop(1, ns, greet_span, 0)
-    lax.fori_loop(1, nf, greet_flow, 0)
+    lax.fori_loop(0, ns - 1, greet_span, 0)
+    lax.fori_loop(0, nf - 1, greet_flow, 0)
 
     row8 = lax.broadcasted_iota(jnp.int32, (8, 128), 0)
     row16 = lax.broadcasted_iota(jnp.int32, (2, 8, 128), 0) * 8 + lax.broadcasted_iota(
@@ -175,13 +182,14 @@
     )
     row32 = lax.broadcasted_iota(jnp.int32, (32, 128), 0)
     lane32 = lax.broadcasted_iota(jnp.int32, (32, 128), 1)
+    lane1 = lax.broadcasted_iota(jnp.int32, (1, 128), 1)
     eye = row32 == lane32
+    loads[5].wait()
     patch = wf_ref[0, 0]
     metal_row = ws_ref[0, 0]
-    coef = wc_ref[0]
+    coef = wc[0]
     wall_mask = jnp.where(row16 == patch, 1.0, 0.0).astype(f32)
     metal_mask = jnp.where(row32 == metal_row, 1.0, 0.0).astype(f32)
-    lane1 = lax.broadcasted_iota(jnp.int32, (1, 128), 1)
     place[pl.ds(f, 1), :] = jnp.where(lane1 == f, metal_row.astype(f32), 0.0)
     has_down = jnp.where(s > 0, 1.0, 0.0).astype(f32)
     has_up = jnp.where(s < ns - 1, 1.0, 0.0).astype(f32)
@@ -189,15 +197,15 @@
     has_right = jnp.where(f < nf - 1, 1.0, 0.0).astype(f32)
 
     def send_rows_flow(buf, k):
-        def one(d, c):
+        def one(i, c):
             pltpu.make_async_remote_copy(
                 src_ref=buf.at[pl.ds(f, 1)], dst_ref=buf.at[pl.ds(f, 1)],
                 send_sem=s_wall.at[k], recv_sem=r_wall.at[k],
-                device_id=(s, lax.rem(f + d, nf)), device_id_type=MESH,
+                device_id=(s, lax.rem(f + far_first(nf, i), nf)), device_id_type=MESH,
             ).start()
             return c
 
-        lax.fori_loop(1, nf, one, 0)
+        lax.fori_loop(0, nf - 1, one, 0)
 
     def rows_flow(buf, k):
         return pltpu.make_async_remote_copy(
@@ -206,15 +214,15 @@
         )
 
     def send_rows_span(buf, k):
-        def one(d, c):
+        def one(i, c):
             pltpu.make_async_remote_copy(
                 src_ref=buf.at[pl.ds(s, 1)], dst_ref=buf.at[pl.ds(s, 1)],
                 send_sem=s_red.at[k], recv_sem=r_red.at[k],
-                device_id=(lax.rem(s + d, ns), f), device_id_type=MESH,
+                device_id=(lax.rem(s + far_first(ns, i), ns), f), device_id_type=MESH,
             ).start()
             return c
 
-        lax.fori_loop(1, ns, one, 0)
+        lax.fori_loop(0, ns - 1, one, 0)
 
     def rows_span(buf, k):
         return pltpu.make_async_remote_copy(
@@ -301,15 +309,20 @@
         above = jnp.where(row32 == 31, has_up * he[k, 1, 0:1, :], pltpu.roll(v, 31, 0))
         return total - below - above
 
-    def dot_row(store, i, j, own_i, own_j):
+    def dot_row(store, i, j):
         total = store[i, 0, 0] * store[j, 0, 0] + store[i, 0, 1] * store[j, 0, 1]
         for g in range(1, 6):
             total = total + store[i, g, 0] * store[j, g, 0] + store[i, g, 1] * store[j, g, 1]
-        return jnp.sum(total, axis=0, keepdims=True) + own_i * own_j
-
-    def packed():
-        sums = jnp.sum(pairs[...], axis=1, keepdims=True)
-        return jnp.sum(jnp.where(eye, sums, 0.0), axis=0, keepdims=True)
+        return jnp.sum(total, axis=0, keepdims=True)
+
+    def metal_dot_row(i, j):
+        t = qm[i] * qm[j]
+        t = (t[0:8] + t[8:16]) + (t[16:24] + t[24:32])
+        return jnp.sum(t, axis=0, keepdims=True)
+
+    def packed(rows, low, high):
+        sums = jnp.sum(rows[low:high, :], axis=1, keepdims=True)
+        return jnp.sum(jnp.where(eye[low:high], sums, 0.0), axis=0, keepdims=True)
 
     def unpack(total):
         sums = jnp.sum(jnp.where(eye, total, 0.0), axis=1, keepdims=True)
@@ -329,6 +342,7 @@
     for copy in edges(0):
         copy.start()
     pairs[...] = jnp.zeros((32, 128), f32)
+    mpairs[...] = jnp.zeros((32, 128), f32)
     loads[2].wait()
     wm[0] = jnp.where(row8 == 0, 0.0, we[2])
     wm[1] = jnp.where(row8 == 7, 0.0, we[3])
@@ -340,23 +354,20 @@
     loads[4].wait()
 
     own = []
-    walls = []
     pick = None
     coef_a = coef_b = None
     for k in range(KRYLOV):
         if k > 0:
             send_halos(k)
         mine = wall_value(k)
-        walls.append(mine)
-        if k < KRYLOV - 1:
-            wall[k, pl.ds(f, 1), :] = mine
-            send_rows_flow(wall.at[k], k)
+        wall[k, pl.ds(f, 1), :] = mine
+        send_rows_flow(wall.at[k], k)
         if k == 0:
-            send_rows_flow(place, KRYLOV - 1)
+            send_rows_flow(place, KRYLOV)
         local_part(k)
         if k > 0:
             if k == 1:
-                rows_flow(place, KRYLOV - 1).wait_recv()
+                rows_flow(place, KRYLOV).wait_recv()
                 places = jnp.sum(place[...], axis=0, keepdims=True)
                 pick = jnp.where((row32.astype(f32) == places) & (lane32 < 32), 1.0, 0.0)[:, 0:32]
             rows_flow(wall.at[k - 1], k - 1).wait_recv()
@@ -373,12 +384,12 @@
             n = 0
             for i in range(EARLY):
                 for j in range(i, EARLY):
-                    pairs[n : n + 1, :] = dot_row(z, i, j, own[i], own[j])
+                    pairs[n : n + 1, :] = dot_row(z, i, j) + own[i] * own[j]
                     n += 1
-            ra[0, pl.ds(f, 1), :] = packed()
-            send_rows_flow(ra.at[0], KRYLOV)
+            ra[0, pl.ds(f, 1), :] = packed(pairs, 0, 32)
+            send_rows_flow(ra.at[0], KRYLOV + 1)
         if k == EARLY:
-            rows_flow(ra.at[0], KRYLOV).wait_recv()
+            rows_flow(ra.at[0], KRYLOV + 1).wait_recv()
             rb[0, pl.ds(s, 1), :] = jnp.sum(ra[0], axis=0, keepdims=True)
             send_rows_span(rb.at[0], 0)
         if k == EARLY + 1:
@@ -441,22 +452,24 @@
                 for j in range(1, i + 1):
                     t = t + jnp.abs(poly[i][j]) * size[j]
                 spread.append(t)
-            qown = []
             for i in range(KRYLOV + 1):
                 for g in range(6):
                     t = poly[i][0] * z[0, g]
                     for j in range(1, min(i, KRYLOV - 1) + 1):
                         t = t + poly[i][j] * z[j, g]
                     q[i, g] = t
-                t = poly[i][0] * own[0]
+                t = poly[i][0] * u[0]
                 for j in range(1, min(i, KRYLOV - 1) + 1):
-                    t = t + poly[i][j] * own[j]
-                qown.append(t)
+                    t = t + poly[i][j] * u[j]
+                qm[i] = t
             n = 0
             for i in range(KRYLOV):
                 for j in range(i + 1):
-                    pairs[n : n + 1, :] = dot_row(q, j, i, qown[j], qown[i])
+                    pairs[n : n + 1, :] = dot_row(q, j, i)
+                    mpairs[n : n + 1, :] = metal_dot_row(j, i)
                     n += 1
+            done = packed(pairs, 0, 24)
+            metal_done = packed(mpairs, 0, 24)
         for copy in halos(k):
             copy.wait_recv()
         halo_part(k, own[k])
@@ -464,28 +477,33 @@
     last = KRYLOV
     for g in range(6):
         q[last, g] = q[last, g] + poly[last][last] * z[last, g]
+    for j in range(last + 1):
+        pairs[24 + j : 25 + j, :] = dot_row(q, j, last)
+    ra[1, pl.ds(f, 1), :] = done + packed(pairs, 24, 32)
+    send_rows_flow(ra.at[1], KRYLOV + 2)
+    rows_flow(wall.at[last - 1], last - 1).wait_recv()
+    sink = jnp.dot(
+        pick, wall[last - 1], precision=lax.Precision.HIGHEST, preferred_element_type=f32
+    )
     for copy in edges(last - 1):
         copy.wait_recv()
-    own_last = own_metal(metal_local(last - 1)) - walls[last - 1]
-    qown[last] = qown[last] + poly[last][last] * own_last
+    qm[last] = qm[last] + poly[last][last] * (metal_local(last - 1) - sink)
     for j in range(last + 1):
-        n = 21 + j
-        pairs[n : n + 1, :] = dot_row(q, j, last, qown[j], qown[last])
-    ra[1, pl.ds(f, 1), :] = packed()
-    send_rows_flow(ra.at[1], KRYLOV + 1)
-    rows_flow(ra.at[1], KRYLOV + 1).wait_recv()
-    rb[1, pl.ds(s, 1), :] = jnp.sum(ra[1], axis=0, keepdims=True)
+        mpairs[24 + j : 25 + j, :] = metal_dot_row(j, last)
+    metal_done = metal_done + packed(mpairs, 24, 32)
+    rows_flow(ra.at[1], KRYLOV + 2).wait_recv()
+    rb[1, pl.ds(s, 1), :] = jnp.sum(ra[1], axis=0, keepdims=True) + metal_done
     send_rows_span(rb.at[1], 1)
     for k in range(KRYLOV):
         for copy in halos(k):
             copy.wait_send()
         for copy in edges(k):
             copy.wait_send()
-    for k in range(KRYLOV - 1):
+    for k in range(KRYLOV):
         rows_flow(wall.at[k], k).wait_send()
-    rows_flow(place, KRYLOV - 1).wait_send()
-    rows_flow(ra.at[0], KRYLOV).wait_send()
-    rows_flow(ra.at[1], KRYLOV + 1).wait_send()
+    rows_flow(place, KRYLOV).wait_send()
+    rows_flow(ra.at[0], KRYLOV + 1).wait_send()
+    rows_flow(ra.at[1], KRYLOV + 2).wait_send()
     rows_span(rb.at[0], 0).wait_send()
     rows_span(rb.at[1], 1).wait()
     unpack(jnp.sum(rb[1], axis=0, keepdims=True))
@@ -493,7 +511,8 @@
     n = 0
     for i in range(KRYLOV + 1):
         for j in range(i + 1):
-            gram[j, i] = scal[n : n + 1, :]
+            m = 24 + j if i == KRYLOV else n
+            gram[j, i] = scal[m : m + 1, :]
             n += 1
     r = {}
     low = None
@@ -543,24 +562,26 @@
 def shards(ns, nf, *args):
     rhs_fluid, rhs_solid = args[0], args[1]
     f32 = jnp.float32
-    hbm = pl.BlockSpec(memory_space=pl.ANY)
+    hbm = pl.BlockSpec(memory_space=pltpu.HBM)
     vmem = pl.BlockSpec(memory_space=pltpu.VMEM)
     smem = pl.BlockSpec(memory_space=pltpu.SMEM)
     dma = pltpu.SemaphoreType.DMA
-    x_fluid, x_solid, ok = pl.pallas_call(
+    x_fluid, x_solid, ok, coef = pl.pallas_call(
         functools.partial(kernel, ns, nf),
         name="gmres",
         out_shape=(
             jax.ShapeDtypeStruct(rhs_fluid.shape, f32),
             jax.ShapeDtypeStruct(rhs_solid.shape, f32),
             jax.ShapeDtypeStruct((1, 128), f32),
+            jax.ShapeDtypeStruct(args[-1].shape, f32),
         ),
-        in_specs=[hbm] * 5 + [smem] * 2 + [vmem],
-        out_specs=(vmem, vmem, vmem),
+        in_specs=[hbm] * 5 + [smem] * 2 + [hbm],
+        out_specs=(vmem,) * 4,
         scratch_shapes=[
             pltpu.VMEM((KRYLOV + 1, 6, 2, 8, 128), f32),
             pltpu.VMEM((KRYLOV, 32, 128), f32),
             pltpu.VMEM((KRYLOV + 1, 6, 2, 8, 128), f32),
+            pltpu.VMEM((KRYLOV + 1, 32, 128), f32),
             pltpu.VMEM((6, 6, 2, 8, 128), f32),
             pltpu.VMEM((6, 2, 8, 128), f32),
             pltpu.VMEM((5, 2, 8, 128), f32),
@@ -569,16 +590,17 @@
             pltpu.VMEM((KRYLOV, 2, 16, 128), f32),
             pltpu.VMEM((KRYLOV, 2, 16, 128), f32),
             pltpu.VMEM((KRYLOV, 2, 8, 128), f32),
-            pltpu.VMEM((KRYLOV - 1, 32, 128), f32),
+            pltpu.VMEM((KRYLOV, 32, 128), f32),
+            pltpu.VMEM((32, 128), f32),
             pltpu.VMEM((32, 128), f32),
             pltpu.VMEM((32, 128), f32),
             pltpu.VMEM((32, 128), f32),
             pltpu.VMEM((2, 32, 128), f32),
             pltpu.VMEM((2, 16, 128), f32),
-            dma((5,)),
+            dma((6,)),
             dma((KRYLOV, 4)), dma((KRYLOV, 4)),
             dma((KRYLOV, 2)), dma((KRYLOV, 2)),
-            dma((KRYLOV + 2,)), dma((KRYLOV + 2,)),
+            dma((KRYLOV + 3,)), dma((KRYLOV + 3,)),
             dma((2,)), dma((2,)),
         ],
         compiler_params=pltpu.CompilerParams(
@@ -586,7 +608,7 @@
         ),
     )(*args)
     return lax.cond(
-        ok[0, 0] > 0.5, lambda *a: (x_fluid, x_solid), lambda *a: arnoldi(*a), *args
+        ok[0, 0] > 0.5, lambda *a: (x_fluid, x_solid), lambda *a: arnoldi(*a), *args[:-1], coef
     )
 
 

time: 60.4 us -> 59.4 us (0.983)
  Pallas kernels: 56.2 us -> 55.1 us
    pallas_call x1, Pallas kernels: 56.2 us -> 55.1 us  [shards(): pl.pallas_call(functools.partial(kernel, ns, nf), name='gmres', out_shape...]
where the time goes in v2:
time: 59.4 us; the launch traced here: 59.1 us
  Pallas kernels  55.1 us (93%)
  between operations  2.1 us (4%)
  local copies, waits for them, and re-layouts  1.88 us (3%)
    pallas_call x1, Pallas kernels, shards(): pl.pallas_call(functools.partial(kernel, ns, nf), name='gmres', out_shape...  55.1 us
    unnamed x14, local copies, waits for them, and re-layouts  1.88 us

profile of v2, /device:TPU:1, one launch (start us, length us, event | category | flops | bytes accessed | tf_op | source)
XLA Modules:
  0.0 59.1 jit_solution(244353276359064202)
XLA Ops:
  1.3 0.0 copy-start
  1.3 0.0 copy-start.2
  2.0 0.0 copy-done
  2.0 0.0 copy-start.1
  2.0 0.0 copy-start.4
  2.0 0.0 copy-start.5
  2.0 55.1 %gmres.1 = (f32[6,2,8,128]{3,2,1,0:T(8,128)S(1)}, f32[32,128]{1,0:T(8,128)S(1)}, f32[1,128]{1,0:T(1,128)S(1)}, f32[1,1,128]{2,1,0:T(1,128)S(1)}) custom-call(f32[6,2,8,128]{3,2,1,0:T(8,128)} %rf_hbm.1, f32[32,128]{1,0:T(8,128)} %rs_hbm.1, f32[6,6,2,8,128]{4,3,2,1,0:T(8,128)} %bl_hbm.1, f32[6,2,8,128]{3,2,1,0:T(8,128)} %we_hbm.1, f32[32,128]{1,0:T(8,128)} %kd_hbm.1, ...), custom_call_target="tpu_custom_call" | custom-call | tf_op jit(solution)/shard_map/gmres/pallas_call | solution.py:569
  57.2 0.0 copy-start.3
  57.2 0.0 copy-done.2
  57.2 0.0 copy-done.1
  57.3 0.0 copy-done.4
  57.3 0.0 copy-done.5
  57.3 0.6 %copy-done.3 = f32[32,128]{1,0:T(8,128)S(1)} copy-done((f32[32,128]{1,0:T(8,128)S(1)}, f32[32,128]{1,0:T(8,128)}, u32[]{:S(2)}) %copy-start.3) | copy-done | bytes 16408
  57.9 0.6 %copy.76 = f32[6,2,8,128]{3,2,1,0:T(8,128)} copy(f32[6,2,8,128]{3,2,1,0:T(8,128)S(1)} %get-tuple-element.295) | data formatting | bytes 98304
  58.5 0.6 %copy.77 = f32[32,128]{1,0:T(8,128)} copy(f32[32,128]{1,0:T(8,128)S(1)} %get-tuple-element.296) | data formatting | bytes 32768
  (1 shorter events, 0.0 us)
Async XLA Ops:
  1.3 0.7 %copy-start = (f32[1,1,128]{2,1,0:T(1,128)S(1)}, f32[1,1,128]{2,1,0:T(1,128)}, u32[]{:S(2)}) copy-start(f32[1,1,128]{2,1,0:T(1,128)} %wc_hbm.1) | copy-start | bytes 1540
  1.3 55.9 %copy-start.2 = (f32[6,6,2,8,128]{4,3,2,1,0:T(8,128)S(1)}, f32[6,6,2,8,128]{4,3,2,1,0:T(8,128)}, u32[]{:S(2)}) copy-start(f32[6,6,2,8,128]{4,3,2,1,0:T(8,128)} %bl_hbm.1) | copy-start | bytes 884740
  2.0 55.2 %copy-start.1 = (f32[6,2,8,128]{3,2,1,0:T(8,128)S(1)}, f32[6,2,8,128]{3,2,1,0:T(8,128)}, u32[]{:S(2)}) copy-start(f32[6,2,8,128]{3,2,1,0:T(8,128)} %rf_hbm.1) | copy-start | bytes 147460
  2.0 55.2 %copy-start.4 = (f32[32,128]{1,0:T(8,128)S(1)}, f32[32,128]{1,0:T(8,128)}, u32[]{:S(2)}) copy-start(f32[32,128]{1,0:T(8,128)} %kd_hbm.1) | copy-start | bytes 49156
  2.0 55.2 %copy-start.5 = (f32[6,2,8,128]{3,2,1,0:T(8,128)S(1)}, f32[6,2,8,128]{3,2,1,0:T(8,128)}, u32[]{:S(2)}) copy-start(f32[6,2,8,128]{3,2,1,0:T(8,128)} %we_hbm.1) | copy-start | bytes 147460
  57.2 0.7 %copy-start.3 = (f32[32,128]{1,0:T(8,128)S(1)}, f32[32,128]{1,0:T(8,128)}, u32[]{:S(2)}) copy-start(f32[32,128]{1,0:T(8,128)} %rs_hbm.1) | copy-start | bytes 49156

commit v3 on v2

--- a/solution.py
+++ b/solution.py
@@ -9,7 +9,10 @@
 
 KRYLOV = 6
 MESH = pl.DeviceIdType.MESH
-EARLY = 4
+EARLY = 3
+PLAN = ((0, 1), (1, 1), (2, 1), (3, 1), (4, 2))
+PAIRS = tuple(k for k, width in PLAN if width == 2)
+CHUNKS = ((0, 2), (2, 4), (4, 6))
 
 
 def extended(shard, sides, width):
@@ -136,7 +139,8 @@
     rf_hbm, rs_hbm, bl_hbm, we_hbm, kd_hbm, wf_ref, ws_ref, wc_hbm,
     xf_ref, xs_ref, ok_ref, wc,
     z, u, q, qm, bl, we, wm, kd, hs, hq, sq, he, wall, place, pairs, mpairs, scal, ra, rb,
-    in_sem, s_halo, r_halo, s_edge, r_edge, s_wall, r_wall, s_red, r_red,
+    tl, th, sb, pk, cb, ir, ib, blo, bhi, bs, pbs, wl, wh, wsr, pws, wn, pid, el, eh, es,
+    in_sem, s_halo, r_halo, s_edge, r_edge, s_wall, r_wall, s_red, r_red, s_pair, r_pair, s_once, r_once,
 ):
     f32 = jnp.float32
     s = lax.axis_index("span")
@@ -145,6 +149,7 @@
     down = (lax.rem(s + ns - 1, ns), f)
     right = (s, lax.rem(f + 1, nf))
     left = (s, lax.rem(f + nf - 1, nf))
+    corners = ((up[0], right[1]), (down[0], right[1]), (up[0], left[1]), (down[0], left[1]))
 
     loads = [
         pltpu.make_async_copy(rf_hbm, z.at[0], in_sem.at[0]),
@@ -157,6 +162,8 @@
     for load in loads:
         load.start()
 
+    cb[...] = jnp.zeros((len(PAIRS), 6, 8, 128), f32)
+
     barrier = pltpu.get_barrier_semaphore()
 
     def far_first(n, i):
@@ -173,6 +180,8 @@
         pl.semaphore_signal(barrier, inc=1, device_id=to, device_id_type=MESH)
         return c
 
+    for to in corners:
+        pl.semaphore_signal(barrier, inc=1, device_id=to, device_id_type=MESH)
     lax.fori_loop(0, ns - 1, greet_span, 0)
     lax.fori_loop(0, nf - 1, greet_flow, 0)
 
@@ -268,6 +277,130 @@
         out[2].start()
         out[3].start()
 
+    def remote(src, dst, send, recv, to):
+        return pltpu.make_async_remote_copy(
+            src_ref=src, dst_ref=dst, send_sem=send, recv_sem=recv, device_id=to, device_id_type=MESH
+        )
+
+    def pair_copies(k):
+        p = PAIRS.index(k)
+
+        def copy(n, src, dst, to):
+            return remote(src, dst, s_pair.at[p, n], r_pair.at[p, n], to)
+
+        return [
+            copy(0, z.at[k], tl.at[p], up),
+            copy(1, z.at[k], th.at[p], down),
+            copy(2, pk.at[p, :, pl.ds(4, 4)], sb.at[p, :, pl.ds(0, 4)], right),
+            copy(3, pk.at[p, :, pl.ds(0, 4)], sb.at[p, :, pl.ds(4, 4)], left),
+            copy(4, pk.at[p, :, pl.ds(5, 1)], cb.at[p, :, pl.ds(0, 1)], corners[0]),
+            copy(5, pk.at[p, :, pl.ds(4, 1)], cb.at[p, :, pl.ds(1, 1)], corners[1]),
+            copy(6, pk.at[p, :, pl.ds(1, 1)], cb.at[p, :, pl.ds(4, 1)], corners[2]),
+            copy(7, pk.at[p, :, pl.ds(0, 1)], cb.at[p, :, pl.ds(5, 1)], corners[3]),
+        ]
+
+    def inflow_copies(k):
+        p = PAIRS.index(k)
+        return [
+            remote(
+                ir.at[p, pl.ds(0, 1)], ib.at[p, pl.ds(n, 1)],
+                s_pair.at[p, 8 + n], r_pair.at[p, 8 + n], to,
+            )
+            for n, to in enumerate((up, down, right, left))
+        ]
+
+    def once_copies(chunk):
+        def copy(n, src, dst, to):
+            return remote(src, dst, s_once.at[n], r_once.at[n], to)
+
+        low, high = CHUNKS[chunk]
+        rows = pl.ds(low, high - low)
+        out = [
+            copy(2 * chunk, bl.at[rows, :, 1], blo.at[rows], up),
+            copy(2 * chunk + 1, bl.at[rows, :, 0], bhi.at[rows], down),
+        ]
+        if chunk == 0:
+            n = 2 * len(CHUNKS)
+            out += [
+                copy(n, we.at[:, 1], wl, up),
+                copy(n + 1, we.at[:, 0], wh, down),
+                copy(n + 2, pbs.at[:, :, pl.ds(4, 4)], bs.at[:, :, pl.ds(0, 4)], right),
+                copy(n + 3, pbs.at[:, :, pl.ds(0, 4)], bs.at[:, :, pl.ds(4, 4)], left),
+                copy(n + 4, pws.at[:, pl.ds(4, 4)], wsr.at[:, pl.ds(0, 4)], right),
+                copy(n + 5, pws.at[:, pl.ds(0, 4)], wsr.at[:, pl.ds(4, 4)], left),
+            ]
+            out += [
+                copy(n + 6 + m, pid.at[pl.ds(4, 1)], pid.at[pl.ds(m, 1)], to)
+                for m, to in enumerate((up, down, right, left))
+            ]
+        return out
+
+    PACK = ((0, 0), (0, 1), (1, 0), (1, 1), (7, 0), (7, 1), (6, 0), (6, 1))
+
+    def pack_once():
+        def one(i, c):
+            for g in range(6):
+                for m, (b, a) in enumerate(PACK):
+                    pbs[i, g, m : m + 1, :] = bl[i, g, a, b : b + 1, :]
+            for m, (b, a) in enumerate(PACK):
+                pws[i, m : m + 1, :] = we[i, a, b : b + 1, :]
+            return c
+
+        lax.fori_loop(0, 6, one, 0)
+        pid[4:5, :] = jnp.broadcast_to(patch.astype(f32), (1, 128))
+
+    def prepare_pairs():
+        wn[0] = wl[2] * jnp.where(row8 == 0, has_left, 1.0)
+        wn[1] = wl[3] * jnp.where(row8 == 7, has_right, 1.0)
+        wn[2] = wh[2] * jnp.where(row8 == 0, has_left, 1.0)
+        wn[3] = wh[3] * jnp.where(row8 == 7, has_right, 1.0)
+        wn[4] = wsr[0] * jnp.where((row8 == 0) | (row8 == 4), has_down, 1.0)
+        wn[5] = wsr[1] * jnp.where((row8 == 1) | (row8 == 5), has_up, 1.0)
+        wn[6] = jnp.where(row8 < 4, wsr[2], wsr[3])
+        wn[7] = jnp.where(row8 < 4, wsr[3], wsr[2])
+        here = row8.astype(f32)
+        wn[8] = jnp.where(here + 8.0 == pid[0:1, :], 1.0, 0.0)
+        wn[9] = jnp.where(here == pid[1:2, :], 1.0, 0.0)
+        side = jnp.where((row8 == 0) & (pid[2:3, :] == 7.0), 1.0, 0.0)
+        side = side + jnp.where((row8 == 1) & (pid[2:3, :] == 15.0), 1.0, 0.0)
+        side = side + jnp.where((row8 == 4) & (pid[3:4, :] == 0.0), 1.0, 0.0)
+        wn[10] = side + jnp.where((row8 == 5) & (pid[3:4, :] == 8.0), 1.0, 0.0)
+
+    def beside_cells(k):
+        p = PAIRS.index(k)
+        odd = (row8 & 1) == 1
+        for g in range(6):
+            v = tl[p, g, 1]
+            total = blo[g, 0] * tl[p, 0, 1]
+            for h in range(1, 6):
+                total = total + blo[g, h] * tl[p, h, 1]
+            total = total - wl[0] * tl[p, g, 0] - wl[1] * z[k, g, 0]
+            total = total - wn[0] * jnp.where(row8 == 0, cb[p, g, 0:1, :], pltpu.roll(v, 1, 0))
+            total = total - wn[1] * jnp.where(row8 == 7, cb[p, g, 4:5, :], pltpu.roll(v, 7, 0))
+            el[g] = total - wl[4] * pltpu.roll(v, 1, 1) - wl[5] * pltpu.roll(v, 127, 1)
+            v = th[p, g, 0]
+            total = bhi[g, 0] * th[p, 0, 0]
+            for h in range(1, 6):
+                total = total + bhi[g, h] * th[p, h, 0]
+            total = total - wh[0] * z[k, g, 1] - wh[1] * th[p, g, 1]
+            total = total - wn[2] * jnp.where(row8 == 0, cb[p, g, 1:2, :], pltpu.roll(v, 1, 0))
+            total = total - wn[3] * jnp.where(row8 == 7, cb[p, g, 5:6, :], pltpu.roll(v, 7, 0))
+            eh[g] = total - wh[4] * pltpu.roll(v, 1, 1) - wh[5] * pltpu.roll(v, 127, 1)
+            v = sb[p, g]
+            total = bs[g, 0] * sb[p, 0]
+            for h in range(1, 6):
+                total = total + bs[g, h] * sb[p, h]
+            total = total - wn[4] * jnp.where(odd, pltpu.roll(v, 1, 0), cb[p, g])
+            total = total - wn[5] * jnp.where(odd, cb[p, g], pltpu.roll(v, 7, 0))
+            total = total - wn[6] * pltpu.roll(v, 6, 0) - wn[7] * pk[p, g]
+            es[g] = total - wsr[4] * pltpu.roll(v, 1, 1) - wsr[5] * pltpu.roll(v, 127, 1)
+
+    def beside_inflow(k):
+        p = PAIRS.index(k)
+        el[5] = el[5] - wn[8] * ib[p, 0:1, :]
+        eh[5] = eh[5] - wn[9] * ib[p, 1:2, :]
+        es[5] = es[5] - wn[10] * jnp.where(row8 < 4, ib[p, 2:3, :], ib[p, 3:4, :])
+
     def local_part(k):
         field = [z[k, g] for g in range(6)]
         for g in range(6):
@@ -280,17 +413,16 @@
             z[k + 1, g, 0] = total[0] - we[1, 0] * v[1]
             z[k + 1, g, 1] = total[1] - we[0, 1] * v[0]
 
-    def halo_part(k, metal_here):
+    def halo_part(k, metal_here, low, high, west, east):
         inflow = coef * metal_here
         for g in range(6):
             for a in range(2):
-                i = 2 * g + a
                 total = z[k + 1, g, a]
                 if a == 0:
-                    total = total - wm[4, 0] * hs[k, 0, g]
+                    total = total - wm[4, 0] * low(g)
                 else:
-                    total = total - wm[4, 1] * hs[k, 1, g]
-                total = total - wm[2, a] * hq[k, 0, i : i + 1, :] - wm[3, a] * hq[k, 1, i : i + 1, :]
+                    total = total - wm[4, 1] * high(g)
+                total = total - wm[2, a] * west(g, a) - wm[3, a] * east(g, a)
                 if g == 5:
                     total = total - wall_mask[a] * inflow
                 z[k + 1, g, a] = total
@@ -335,7 +467,7 @@
             sq[0, 0, i : i + 1, :] = z[0, g, a, 7:8, :]
             sq[0, 1, i : i + 1, :] = z[0, g, a, 0:1, :]
     sq[:, :, 12:16, :] = jnp.zeros((KRYLOV, 2, 4, 128), f32)
-    pl.semaphore_wait(barrier, ns + nf - 2)
+    pl.semaphore_wait(barrier, ns + nf + 2)
     for copy in halos(0):
         copy.start()
     loads[1].wait()
@@ -354,25 +486,22 @@
     loads[4].wait()
 
     own = []
-    pick = None
-    coef_a = coef_b = None
-    for k in range(KRYLOV):
+    state = {}
+
+    def wall_step(k):
+        wall[k, pl.ds(f, 1), :] = wall_value(k)
+        send_rows_flow(wall.at[k], k)
+
+    def metal_step(k):
+        if k == 1:
+            rows_flow(place, KRYLOV).wait_recv()
+            places = jnp.sum(place[...], axis=0, keepdims=True)
+            state["pick"] = jnp.where((row32.astype(f32) == places) & (lane32 < 32), 1.0, 0.0)[:, 0:32]
         if k > 0:
-            send_halos(k)
-        mine = wall_value(k)
-        wall[k, pl.ds(f, 1), :] = mine
-        send_rows_flow(wall.at[k], k)
-        if k == 0:
-            send_rows_flow(place, KRYLOV)
-        local_part(k)
-        if k > 0:
-            if k == 1:
-                rows_flow(place, KRYLOV).wait_recv()
-                places = jnp.sum(place[...], axis=0, keepdims=True)
-                pick = jnp.where((row32.astype(f32) == places) & (lane32 < 32), 1.0, 0.0)[:, 0:32]
             rows_flow(wall.at[k - 1], k - 1).wait_recv()
             sink = jnp.dot(
-                pick, wall[k - 1], precision=lax.Precision.HIGHEST, preferred_element_type=f32
+                state["pick"], wall[k - 1],
+                precision=lax.Precision.HIGHEST, preferred_element_type=f32,
             )
             for copy in edges(k - 1):
                 copy.wait_recv()
@@ -380,123 +509,221 @@
             for copy in edges(k):
                 copy.start()
         own.append(own_metal(u[k]))
-        if k == EARLY - 1:
-            n = 0
-            for i in range(EARLY):
-                for j in range(i, EARLY):
-                    pairs[n : n + 1, :] = dot_row(z, i, j) + own[i] * own[j]
-                    n += 1
-            ra[0, pl.ds(f, 1), :] = packed(pairs, 0, 32)
-            send_rows_flow(ra.at[0], KRYLOV + 1)
-        if k == EARLY:
-            rows_flow(ra.at[0], KRYLOV + 1).wait_recv()
-            rb[0, pl.ds(s, 1), :] = jnp.sum(ra[0], axis=0, keepdims=True)
-            send_rows_span(rb.at[0], 0)
-        if k == EARLY + 1:
-            rows_span(rb.at[0], 0).wait_recv()
-            unpack(jnp.sum(rb[0], axis=0, keepdims=True))
-            gram = {}
-            n = 0
-            for i in range(EARLY):
-                for j in range(i, EARLY):
-                    gram[i, j] = scal[n : n + 1, :]
-                    n += 1
-            r = {}
-            inv = []
-            trust = []
-            for i in range(EARLY):
-                for j in range(i, EARLY):
-                    t = gram[i, j]
-                    for h in range(i):
-                        t = t - r[h, i] * r[h, j]
-                    if i == j:
-                        floor = gram[i, i] * 1e-5
-                        trust.append(t > floor)
-                        t = jnp.maximum(t, floor)
-                        inv.append(lax.rsqrt(t))
-                    r[i, j] = t * inv[i]
-            ratio = [r[i, i + 1] * inv[i] for i in range(EARLY - 1)]
-            coef_a = [ratio[0]]
-            coef_b = [None, r[1, 1] * inv[0]]
-            good = trust[1]
-            for i in range(1, EARLY - 1):
-                good = good & trust[i + 1]
-                coef_a.append(jnp.where(good, ratio[i] - ratio[i - 1], coef_a[i - 1]))
-                guess = coef_b[1] * 1.22
-                coef_b.append(jnp.where(good, r[i + 1, i + 1] * inv[i], guess))
-            while len(coef_a) < KRYLOV:
-                coef_a.append(coef_a[-1])
-            while len(coef_b) < KRYLOV + 1:
-                coef_b.append(coef_b[-1])
-            poly = [[inv[0]]]
-            for i in range(KRYLOV):
-                back = 1.0 / coef_b[i + 1]
-                new = []
-                for j in range(i + 2):
-                    t = None
-                    if j >= 1:
-                        t = poly[i][j - 1]
-                    if j <= i:
-                        t = -coef_a[i] * poly[i][j] if t is None else t - coef_a[i] * poly[i][j]
-                    if i >= 1 and j <= i - 1:
-                        t = t - coef_b[i] * poly[i - 1][j]
-                    new.append(t * back)
-                poly.append(new)
-            size = [jnp.sqrt(gram[i, i]) for i in range(EARLY)]
-            growth = size[-1] / size[-2]
-            while len(size) < KRYLOV:
-                size.append(size[-1] * growth)
-            spread = []
-            for i in range(KRYLOV):
-                t = jnp.abs(poly[i][0]) * size[0]
-                for j in range(1, i + 1):
-                    t = t + jnp.abs(poly[i][j]) * size[j]
-                spread.append(t)
-            for i in range(KRYLOV + 1):
+
+    def early_gram():
+        n = 0
+        for i in range(EARLY):
+            for j in range(i, EARLY):
+                pairs[n : n + 1, :] = dot_row(z, i, j) + own[i] * own[j]
+                n += 1
+        ra[0, pl.ds(f, 1), :] = packed(pairs, 0, 32)
+        send_rows_flow(ra.at[0], KRYLOV + 1)
+
+    def early_span():
+        rows_flow(ra.at[0], KRYLOV + 1).wait_recv()
+        rb[0, pl.ds(s, 1), :] = jnp.sum(ra[0], axis=0, keepdims=True)
+        send_rows_span(rb.at[0], 0)
+
+    def basis():
+        rows_span(rb.at[0], 0).wait_recv()
+        unpack(jnp.sum(rb[0], axis=0, keepdims=True))
+        gram = {}
+        n = 0
+        for i in range(EARLY):
+            for j in range(i, EARLY):
+                gram[i, j] = scal[n : n + 1, :]
+                n += 1
+        r = {}
+        inv = []
+        trust = []
+        for i in range(EARLY):
+            for j in range(i, EARLY):
+                t = gram[i, j]
+                for h in range(i):
+                    t = t - r[h, i] * r[h, j]
+                if i == j:
+                    floor = gram[i, i] * 1e-5
+                    trust.append(t > floor)
+                    t = jnp.maximum(t, floor)
+                    inv.append(lax.rsqrt(t))
+                r[i, j] = t * inv[i]
+        ratio = [r[i, i + 1] * inv[i] for i in range(EARLY - 1)]
+        coef_a = [ratio[0]]
+        coef_b = [None, r[1, 1] * inv[0]]
+        good = trust[1]
+        for i in range(1, EARLY - 1):
+            good = good & trust[i + 1]
+            coef_a.append(jnp.where(good, ratio[i] - ratio[i - 1], coef_a[i - 1]))
+            guess = coef_b[1] * 1.22
+            coef_b.append(jnp.where(good, r[i + 1, i + 1] * inv[i], guess))
+        while len(coef_a) < KRYLOV:
+            coef_a.append(coef_a[-1])
+        while len(coef_b) < KRYLOV + 1:
+            coef_b.append(coef_b[-1])
+        poly = [[inv[0]]]
+        for i in range(KRYLOV):
+            back = 1.0 / coef_b[i + 1]
+            new = []
+            for j in range(i + 2):
+                t = None
+                if j >= 1:
+                    t = poly[i][j - 1]
+                if j <= i:
+                    t = -coef_a[i] * poly[i][j] if t is None else t - coef_a[i] * poly[i][j]
+                if i >= 1 and j <= i - 1:
+                    t = t - coef_b[i] * poly[i - 1][j]
+                new.append(t * back)
+            poly.append(new)
+        size = [jnp.sqrt(gram[i, i]) for i in range(EARLY)]
+        growth = size[-1] / size[-2]
+        while len(size) < KRYLOV:
+            size.append(size[-1] * growth)
+        spread = []
+        for i in range(KRYLOV):
+            t = jnp.abs(poly[i][0]) * size[0]
+            for j in range(1, i + 1):
+                t = t + jnp.abs(poly[i][j]) * size[j]
+            spread.append(t)
+        return coef_a, coef_b, poly, spread
+
+    def combine(low, high, first):
+        poly = state["basis"][2]
+        for i in range(low, KRYLOV + 1):
+            terms = range(low, min(i, high) + 1)
+            if not terms:
+                continue
+            for g in range(6):
+                t = None if first else q[i, g]
+                for j in terms:
+                    t = poly[i][j] * z[j, g] if t is None else t + poly[i][j] * z[j, g]
+                q[i, g] = t
+
+    def metal_combine(low, high, first):
+        poly = state["basis"][2]
+        for i in range(low, KRYLOV + 1):
+            t = None if first else qm[i]
+            for j in range(low, min(i, high) + 1):
+                t = poly[i][j] * u[j] if t is None else t + poly[i][j] * u[j]
+            qm[i] = t
+
+    def place_of(j, i):
+        return 24 + j if i == KRYLOV else i * (i + 1) // 2 + j
+
+    def gram_rows(low, high):
+        for i in range(low, high + 1):
+            for j in range(i + 1):
+                n = place_of(j, i)
+                pairs[n : n + 1, :] = dot_row(q, j, i)
+
+    def metal_gram_rows(low, high):
+        for i in range(low, high + 1):
+            for j in range(i + 1):
+                n = place_of(j, i)
+                mpairs[n : n + 1, :] = metal_dot_row(j, i)
+
+    early = [k for k, _ in PLAN if k >= EARLY - 1][0]
+    when = [k for k, _ in PLAN].index(early)
+    for step, (k, width) in enumerate(PLAN):
+        if k > 0:
+            if width == 1:
+                send_halos(k)
+            else:
+                p = PAIRS.index(k)
+                copies = pair_copies(k)
+                copies[0].start()
+                copies[1].start()
                 for g in range(6):
-                    t = poly[i][0] * z[0, g]
-                    for j in range(1, min(i, KRYLOV - 1) + 1):
-                        t = t + poly[i][j] * z[j, g]
-                    q[i, g] = t
-                t = poly[i][0] * u[0]
-                for j in range(1, min(i, KRYLOV - 1) + 1):
-                    t = t + poly[i][j] * u[j]
-                qm[i] = t
-            n = 0
-            for i in range(KRYLOV):
-                for j in range(i + 1):
-                    pairs[n : n + 1, :] = dot_row(q, j, i)
-                    mpairs[n : n + 1, :] = metal_dot_row(j, i)
-                    n += 1
-            done = packed(pairs, 0, 24)
-            metal_done = packed(mpairs, 0, 24)
-        for copy in halos(k):
-            copy.wait_recv()
-        halo_part(k, own[k])
+                    for m, (b, a) in enumerate(PACK):
+                        pk[p, g, m : m + 1, :] = z[k, g, a, b : b + 1, :]
+                for copy in copies[4:] + copies[2:4]:
+                    copy.start()
+        wall_step(k)
+        if k == 0:
+            send_rows_flow(place, KRYLOV)
+        local_part(k)
+        metal_step(k)
+        if width == 2:
+            p = PAIRS.index(k)
+            ir[p, 0:1, :] = coef * own[k]
+            for copy in inflow_copies(k):
+                copy.start()
+        if step == 0:
+            pack_once()
+        if step < len(CHUNKS):
+            for copy in once_copies(step):
+                copy.start()
+        if step == when:
+            early_gram()
+        if step == when + 1:
+            early_span()
+        if step == when + 2:
+            state["basis"] = basis()
+            combine(0, k, True)
+            gram_rows(0, k)
+        if width == 1:
+            for copy in halos(k):
+                copy.wait_recv()
+            halo_part(
+                k, own[k], lambda g: hs[k, 0, g], lambda g: hs[k, 1, g],
+                lambda g, a: hq[k, 0, 2 * g + a : 2 * g + a + 1, :],
+                lambda g, a: hq[k, 1, 2 * g + a : 2 * g + a + 1, :],
+            )
+        else:
+            if k == PAIRS[0]:
+                for chunk in range(len(CHUNKS)):
+                    for copy in once_copies(chunk):
+                        copy.wait_recv()
+                prepare_pairs()
+            for copy in pair_copies(k):
+                copy.wait_recv()
+            halo_part(
+                k, own[k], lambda g: tl[p, g, 1], lambda g: th[p, g, 0],
+                lambda g, a: sb[p, g, a : a + 1, :],
+                lambda g, a: sb[p, g, 4 + a : 5 + a, :],
+            )
+            wall_step(k + 1)
+            beside_cells(k)
+            local_part(k + 1)
+            if k + 1 == KRYLOV - 1:
+                combine(k + 1, k + 1, False)
+                gram_rows(k + 1, k + 1)
+            for copy in inflow_copies(k):
+                copy.wait_recv()
+            beside_inflow(k)
+            metal_step(k + 1)
+            halo_part(
+                k + 1, own[k + 1], lambda g: el[g], lambda g: eh[g],
+                lambda g, a: es[g, a : a + 1, :],
+                lambda g, a: es[g, 4 + a : 5 + a, :],
+            )
 
     last = KRYLOV
-    for g in range(6):
-        q[last, g] = q[last, g] + poly[last][last] * z[last, g]
-    for j in range(last + 1):
-        pairs[24 + j : 25 + j, :] = dot_row(q, j, last)
-    ra[1, pl.ds(f, 1), :] = done + packed(pairs, 24, 32)
+    combine(last, last, False)
+    gram_rows(last, last)
+    ra[1, pl.ds(f, 1), :] = packed(pairs, 0, 32)
     send_rows_flow(ra.at[1], KRYLOV + 2)
+    coef_a, coef_b, poly, spread = state["basis"]
+    metal_combine(0, last - 1, True)
+    metal_gram_rows(0, last - 1)
     rows_flow(wall.at[last - 1], last - 1).wait_recv()
     sink = jnp.dot(
-        pick, wall[last - 1], precision=lax.Precision.HIGHEST, preferred_element_type=f32
+        state["pick"], wall[last - 1], precision=lax.Precision.HIGHEST, preferred_element_type=f32
     )
     for copy in edges(last - 1):
         copy.wait_recv()
     qm[last] = qm[last] + poly[last][last] * (metal_local(last - 1) - sink)
-    for j in range(last + 1):
-        mpairs[24 + j : 25 + j, :] = metal_dot_row(j, last)
-    metal_done = metal_done + packed(mpairs, 24, 32)
+    metal_gram_rows(last, last)
+    metal_done = packed(mpairs, 0, 32)
     rows_flow(ra.at[1], KRYLOV + 2).wait_recv()
     rb[1, pl.ds(s, 1), :] = jnp.sum(ra[1], axis=0, keepdims=True) + metal_done
     send_rows_span(rb.at[1], 1)
+    for k, width in PLAN:
+        for copy in halos(k) if width == 1 else pair_copies(k) + inflow_copies(k):
+            copy.wait_send()
+    for chunk in range(len(CHUNKS)):
+        for copy in once_copies(chunk):
+            copy.wait_send()
     for k in range(KRYLOV):
-        for copy in halos(k):
-            copy.wait_send()
         for copy in edges(k):
             copy.wait_send()
     for k in range(KRYLOV):
@@ -597,11 +824,33 @@
             pltpu.VMEM((32, 128), f32),
             pltpu.VMEM((2, 32, 128), f32),
             pltpu.VMEM((2, 16, 128), f32),
+            pltpu.VMEM((len(PAIRS), 6, 2, 8, 128), f32),
+            pltpu.VMEM((len(PAIRS), 6, 2, 8, 128), f32),
+            pltpu.VMEM((len(PAIRS), 6, 8, 128), f32),
+            pltpu.VMEM((len(PAIRS), 6, 8, 128), f32),
+            pltpu.VMEM((len(PAIRS), 6, 8, 128), f32),
+            pltpu.VMEM((len(PAIRS), 8, 128), f32),
+            pltpu.VMEM((len(PAIRS), 8, 128), f32),
+            pltpu.VMEM((6, 6, 8, 128), f32),
+            pltpu.VMEM((6, 6, 8, 128), f32),
+            pltpu.VMEM((6, 6, 8, 128), f32),
+            pltpu.VMEM((6, 6, 8, 128), f32),
+            pltpu.VMEM((6, 8, 128), f32),
+            pltpu.VMEM((6, 8, 128), f32),
+            pltpu.VMEM((6, 8, 128), f32),
+            pltpu.VMEM((6, 8, 128), f32),
+            pltpu.VMEM((11, 8, 128), f32),
+            pltpu.VMEM((8, 128), f32),
+            pltpu.VMEM((6, 8, 128), f32),
+            pltpu.VMEM((6, 8, 128), f32),
+            pltpu.VMEM((6, 8, 128), f32),
             dma((6,)),
             dma((KRYLOV, 4)), dma((KRYLOV, 4)),
             dma((KRYLOV, 2)), dma((KRYLOV, 2)),
             dma((KRYLOV + 3,)), dma((KRYLOV + 3,)),
             dma((2,)), dma((2,)),
+            dma((len(PAIRS), 12)), dma((len(PAIRS), 12)),
+            dma((2 * len(CHUNKS) + 10,)), dma((2 * len(CHUNKS) + 10,)),
         ],
         compiler_params=pltpu.CompilerParams(
             collective_id=0, has_side_effects=True, vmem_limit_bytes=8 * 1024 * 1024

time: 59.4 us -> 59.7 us (level)
  no operation moved by 1% of the time
where the time goes in v3:
time: 59.7 us; the launch traced here: 59.5 us
  Pallas kernels  55.5 us (93%)
  between operations  2.1 us (4%)
  local copies, waits for them, and re-layouts  1.88 us (3%)
    pallas_call x1, Pallas kernels, shards(): pl.pallas_call(functools.partial(kernel, ns, nf), name='gmres', out_shape...  55.5 us
    unnamed x14, local copies, waits for them, and re-layouts  1.88 us

profile of v3, /device:TPU:1, one launch (start us, length us, event | category | flops | bytes accessed | tf_op | source)
XLA Modules:
  0.0 59.5 jit_solution(7558014975164290407)
XLA Ops:
  1.3 0.0 copy-start
  1.3 0.0 copy-start.2
  2.0 0.0 copy-done
  2.0 0.0 copy-start.1
  2.0 0.0 copy-start.4
  2.0 0.0 copy-start.5
  2.0 55.5 %gmres.1 = (f32[6,2,8,128]{3,2,1,0:T(8,128)S(1)}, f32[32,128]{1,0:T(8,128)S(1)}, f32[1,128]{1,0:T(1,128)S(1)}, f32[1,1,128]{2,1,0:T(1,128)S(1)}) custom-call(f32[6,2,8,128]{3,2,1,0:T(8,128)} %rf_hbm.1, f32[32,128]{1,0:T(8,128)} %rs_hbm.1, f32[6,6,2,8,128]{4,3,2,1,0:T(8,128)} %bl_hbm.1, f32[6,2,8,128]{3,2,1,0:T(8,128)} %we_hbm.1, f32[32,128]{1,0:T(8,128)} %kd_hbm.1, ...), custom_call_target="tpu_custom_call" | custom-call | tf_op jit(solution)/shard_map/gmres/pallas_call | solution.py:796
  57.5 0.0 copy-start.3
  57.6 0.0 copy-done.2
  57.6 0.0 copy-done.1
  57.6 0.0 copy-done.4
  57.6 0.0 copy-done.5
  57.6 0.6 %copy-done.3 = f32[32,128]{1,0:T(8,128)S(1)} copy-done((f32[32,128]{1,0:T(8,128)S(1)}, f32[32,128]{1,0:T(8,128)}, u32[]{:S(2)}) %copy-start.3) | copy-done | bytes 16408
  58.2 0.6 %copy.76 = f32[6,2,8,128]{3,2,1,0:T(8,128)} copy(f32[6,2,8,128]{3,2,1,0:T(8,128)S(1)} %get-tuple-element.295) | data formatting | bytes 98304
  58.8 0.6 %copy.77 = f32[32,128]{1,0:T(8,128)} copy(f32[32,128]{1,0:T(8,128)S(1)} %get-tuple-element.296) | data formatting | bytes 32768
  (1 shorter events, 0.0 us)
Async XLA Ops:
  1.3 0.7 %copy-start = (f32[1,1,128]{2,1,0:T(1,128)S(1)}, f32[1,1,128]{2,1,0:T(1,128)}, u32[]{:S(2)}) copy-start(f32[1,1,128]{2,1,0:T(1,128)} %wc_hbm.1) | copy-start | bytes 1540
  1.3 56.3 %copy-start.2 = (f32[6,6,2,8,128]{4,3,2,1,0:T(8,128)S(1)}, f32[6,6,2,8,128]{4,3,2,1,0:T(8,128)}, u32[]{:S(2)}) copy-start(f32[6,6,2,8,128]{4,3,2,1,0:T(8,128)} %bl_hbm.1) | copy-start | bytes 884740
  2.0 55.6 %copy-start.1 = (f32[6,2,8,128]{3,2,1,0:T(8,128)S(1)}, f32[6,2,8,128]{3,2,1,0:T(8,128)}, u32[]{:S(2)}) copy-start(f32[6,2,8,128]{3,2,1,0:T(8,128)} %rf_hbm.1) | copy-start | bytes 147460
  2.0 55.6 %copy-start.4 = (f32[32,128]{1,0:T(8,128)S(1)}, f32[32,128]{1,0:T(8,128)}, u32[]{:S(2)}) copy-start(f32[32,128]{1,0:T(8,128)} %kd_hbm.1) | copy-start | bytes 49156
  2.0 55.6 %copy-start.5 = (f32[6,2,8,128]{3,2,1,0:T(8,128)S(1)}, f32[6,2,8,128]{3,2,1,0:T(8,128)}, u32[]{:S(2)}) copy-start(f32[6,2,8,128]{3,2,1,0:T(8,128)} %we_hbm.1) | copy-start | bytes 147460
  57.5 0.7 %copy-start.3 = (f32[32,128]{1,0:T(8,128)S(1)}, f32[32,128]{1,0:T(8,128)}, u32[]{:S(2)}) copy-start(f32[32,128]{1,0:T(8,128)} %rs_hbm.1) | copy-start | bytes 49156

commit v4 on v3

--- a/solution.py
+++ b/solution.py
@@ -9,10 +9,10 @@
 
 KRYLOV = 6
 MESH = pl.DeviceIdType.MESH
-EARLY = 3
+EARLY = 2
 PLAN = ((0, 1), (1, 1), (2, 1), (3, 1), (4, 2))
 PAIRS = tuple(k for k, width in PLAN if width == 2)
-CHUNKS = ((0, 2), (2, 4), (4, 6))
+CHUNKS = ((0, 1), (1, 3), (3, 5), (5, 6))
 
 
 def extended(shard, sides, width):
@@ -166,25 +166,15 @@
 
     barrier = pltpu.get_barrier_semaphore()
 
-    def far_first(n, i):
-        half = lax.div(i + 1, 2)
-        return n // 2 + jnp.where(lax.rem(i, 2) == 1, half, -half)
-
-    def greet_flow(i, c):
-        to = (s, lax.rem(f + far_first(nf, i), nf))
+    def far_first(n):
+        return sorted(range(1, n), key=lambda d: -min(d, n - d))
+
+    flow_peers = [(s, lax.rem(f + d, nf)) for d in far_first(nf)]
+    span_peers = [(lax.rem(s + d, ns), f) for d in far_first(ns)]
+    for to in span_peers + flow_peers:
         pl.semaphore_signal(barrier, inc=1, device_id=to, device_id_type=MESH)
-        return c
-
-    def greet_span(i, c):
-        to = (lax.rem(s + far_first(ns, i), ns), f)
-        pl.semaphore_signal(barrier, inc=1, device_id=to, device_id_type=MESH)
-        return c
-
     for to in corners:
         pl.semaphore_signal(barrier, inc=1, device_id=to, device_id_type=MESH)
-    lax.fori_loop(0, ns - 1, greet_span, 0)
-    lax.fori_loop(0, nf - 1, greet_flow, 0)
-
     row8 = lax.broadcasted_iota(jnp.int32, (8, 128), 0)
     row16 = lax.broadcasted_iota(jnp.int32, (2, 8, 128), 0) * 8 + lax.broadcasted_iota(
         jnp.int32, (2, 8, 128), 1
@@ -206,15 +196,11 @@
     has_right = jnp.where(f < nf - 1, 1.0, 0.0).astype(f32)
 
     def send_rows_flow(buf, k):
-        def one(i, c):
+        for to in flow_peers:
             pltpu.make_async_remote_copy(
                 src_ref=buf.at[pl.ds(f, 1)], dst_ref=buf.at[pl.ds(f, 1)],
-                send_sem=s_wall.at[k], recv_sem=r_wall.at[k],
-                device_id=(s, lax.rem(f + far_first(nf, i), nf)), device_id_type=MESH,
+                send_sem=s_wall.at[k], recv_sem=r_wall.at[k], device_id=to, device_id_type=MESH,
             ).start()
-            return c
-
-        lax.fori_loop(0, nf - 1, one, 0)
 
     def rows_flow(buf, k):
         return pltpu.make_async_remote_copy(
@@ -223,15 +209,11 @@
         )
 
     def send_rows_span(buf, k):
-        def one(i, c):
+        for to in span_peers:
             pltpu.make_async_remote_copy(
                 src_ref=buf.at[pl.ds(s, 1)], dst_ref=buf.at[pl.ds(s, 1)],
-                send_sem=s_red.at[k], recv_sem=r_red.at[k],
-                device_id=(lax.rem(s + far_first(ns, i), ns), f), device_id_type=MESH,
+                send_sem=s_red.at[k], recv_sem=r_red.at[k], device_id=to, device_id_type=MESH,
             ).start()
-            return c
-
-        lax.fori_loop(0, ns - 1, one, 0)
 
     def rows_span(buf, k):
         return pltpu.make_async_remote_copy(
@@ -324,8 +306,8 @@
             out += [
                 copy(n, we.at[:, 1], wl, up),
                 copy(n + 1, we.at[:, 0], wh, down),
-                copy(n + 2, pbs.at[:, :, pl.ds(4, 4)], bs.at[:, :, pl.ds(0, 4)], right),
-                copy(n + 3, pbs.at[:, :, pl.ds(0, 4)], bs.at[:, :, pl.ds(4, 4)], left),
+                copy(n + 2, pbs.at[:, :, pl.ds(4, 2)], bs.at[:, :, pl.ds(0, 2)], right),
+                copy(n + 3, pbs.at[:, :, pl.ds(0, 2)], bs.at[:, :, pl.ds(4, 2)], left),
                 copy(n + 4, pws.at[:, pl.ds(4, 4)], wsr.at[:, pl.ds(0, 4)], right),
                 copy(n + 5, pws.at[:, pl.ds(0, 4)], wsr.at[:, pl.ds(4, 4)], left),
             ]
@@ -514,7 +496,7 @@
         n = 0
         for i in range(EARLY):
             for j in range(i, EARLY):
-                pairs[n : n + 1, :] = dot_row(z, i, j) + own[i] * own[j]
+                pairs[n : n + 1, :] = dot_row(z, i, j)
                 n += 1
         ra[0, pl.ds(f, 1), :] = packed(pairs, 0, 32)
         send_rows_flow(ra.at[0], KRYLOV + 1)
@@ -637,9 +619,15 @@
                         pk[p, g, m : m + 1, :] = z[k, g, a, b : b + 1, :]
                 for copy in copies[4:] + copies[2:4]:
                     copy.start()
+        if step == when:
+            early_gram()
         wall_step(k)
         if k == 0:
             send_rows_flow(place, KRYLOV)
+            pack_once()
+        if step < len(CHUNKS):
+            for copy in once_copies(step):
+                copy.start()
         local_part(k)
         metal_step(k)
         if width == 2:
@@ -647,16 +635,9 @@
             ir[p, 0:1, :] = coef * own[k]
             for copy in inflow_copies(k):
                 copy.start()
-        if step == 0:
-            pack_once()
-        if step < len(CHUNKS):
-            for copy in once_copies(step):
-                copy.start()
-        if step == when:
-            early_gram()
         if step == when + 1:
             early_span()
-        if step == when + 2:
+        if step == when + 3:
             state["basis"] = basis()
             combine(0, k, True)
             gram_rows(0, k)

time: 59.7 us -> 57.8 us (0.968)
  Pallas kernels: 55.5 us -> 53.6 us
    pallas_call x1, Pallas kernels: 55.5 us -> 53.6 us  [shards(): pl.pallas_call(functools.partial(kernel, ns, nf), name='gmres', out_shape...]
where the time goes in v4:
time: 57.8 us; the launch traced here: 57.6 us
  Pallas kernels  53.6 us (93%)
  between operations  2.1 us (4%)
  local copies, waits for them, and re-layouts  1.88 us (3%)
    pallas_call x1, Pallas kernels, shards(): pl.pallas_call(functools.partial(kernel, ns, nf), name='gmres', out_shape...  53.6 us
    unnamed x14, local copies, waits for them, and re-layouts  1.88 us

profile of v4, /device:TPU:1, one launch (start us, length us, event | category | flops | bytes accessed | tf_op | source)
XLA Modules:
  0.0 57.6 jit_solution(13237592273897995951)
XLA Ops:
  1.3 0.0 copy-start
  1.3 0.0 copy-start.2
  2.0 0.0 copy-done
  2.0 0.0 copy-start.1
  2.0 0.0 copy-start.4
  2.0 0.0 copy-start.5
  2.0 53.6 %gmres.1 = (f32[6,2,8,128]{3,2,1,0:T(8,128)S(1)}, f32[32,128]{1,0:T(8,128)S(1)}, f32[1,128]{1,0:T(1,128)S(1)}, f32[1,1,128]{2,1,0:T(1,128)S(1)}) custom-call(f32[6,2,8,128]{3,2,1,0:T(8,128)} %rf_hbm.1, f32[32,128]{1,0:T(8,128)} %rs_hbm.1, f32[6,6,2,8,128]{4,3,2,1,0:T(8,128)} %bl_hbm.1, f32[6,2,8,128]{3,2,1,0:T(8,128)} %we_hbm.1, f32[32,128]{1,0:T(8,128)} %kd_hbm.1, ...), custom_call_target="tpu_custom_call" | custom-call | tf_op jit(solution)/shard_map/gmres/pallas_call | solution.py:777
  55.6 0.0 copy-start.3
  55.7 0.0 copy-done.2
  55.7 0.0 copy-done.1
  55.7 0.0 copy-done.4
  55.7 0.0 copy-done.5
  55.7 0.6 %copy-done.3 = f32[32,128]{1,0:T(8,128)S(1)} copy-done((f32[32,128]{1,0:T(8,128)S(1)}, f32[32,128]{1,0:T(8,128)}, u32[]{:S(2)}) %copy-start.3) | copy-done | bytes 16408
  56.4 0.6 %copy.76 = f32[6,2,8,128]{3,2,1,0:T(8,128)} copy(f32[6,2,8,128]{3,2,1,0:T(8,128)S(1)} %get-tuple-element.295) | data formatting | bytes 98304
  57.0 0.6 %copy.77 = f32[32,128]{1,0:T(8,128)} copy(f32[32,128]{1,0:T(8,128)S(1)} %get-tuple-element.296) | data formatting | bytes 32768
  (1 shorter events, 0.0 us)
Async XLA Ops:
  1.3 0.7 %copy-start = (f32[1,1,128]{2,1,0:T(1,128)S(1)}, f32[1,1,128]{2,1,0:T(1,128)}, u32[]{:S(2)}) copy-start(f32[1,1,128]{2,1,0:T(1,128)} %wc_hbm.1) | copy-start | bytes 1540
  1.3 54.4 %copy-start.2 = (f32[6,6,2,8,128]{4,3,2,1,0:T(8,128)S(1)}, f32[6,6,2,8,128]{4,3,2,1,0:T(8,128)}, u32[]{:S(2)}) copy-start(f32[6,6,2,8,128]{4,3,2,1,0:T(8,128)} %bl_hbm.1) | copy-start | bytes 884740
  2.0 53.7 %copy-start.1 = (f32[6,2,8,128]{3,2,1,0:T(8,128)S(1)}, f32[6,2,8,128]{3,2,1,0:T(8,128)}, u32[]{:S(2)}) copy-start(f32[6,2,8,128]{3,2,1,0:T(8,128)} %rf_hbm.1) | copy-start | bytes 147460
  2.0 53.7 %copy-start.4 = (f32[32,128]{1,0:T(8,128)S(1)}, f32[32,128]{1,0:T(8,128)}, u32[]{:S(2)}) copy-start(f32[32,128]{1,0:T(8,128)} %kd_hbm.1) | copy-start | bytes 49156
  2.0 53.7 %copy-start.5 = (f32[6,2,8,128]{3,2,1,0:T(8,128)S(1)}, f32[6,2,8,128]{3,2,1,0:T(8,128)}, u32[]{:S(2)}) copy-start(f32[6,2,8,128]{3,2,1,0:T(8,128)} %we_hbm.1) | copy-start | bytes 147460
  55.6 0.7 %copy-start.3 = (f32[32,128]{1,0:T(8,128)S(1)}, f32[32,128]{1,0:T(8,128)}, u32[]{:S(2)}) copy-start(f32[32,128]{1,0:T(8,128)} %rs_hbm.1) | copy-start | bytes 49156

commit v5 on v4

--- a/solution.py
+++ b/solution.py
@@ -12,7 +12,6 @@
 EARLY = 2
 PLAN = ((0, 1), (1, 1), (2, 1), (3, 1), (4, 2))
 PAIRS = tuple(k for k, width in PLAN if width == 2)
-CHUNKS = ((0, 1), (1, 3), (3, 5), (5, 6))
 
 
 def extended(shard, sides, width):
@@ -134,12 +133,39 @@
     return (x_fluid, x_solid)
 
 
+def small_solve(hess, beta, zero, steps):
+    cos_list, sin_list, upper, inverse = ([], [], [], [])
+    rhs_g = [beta] + [zero for _ in range(steps)]
+    for j in range(steps):
+        column = [hess[i][j] for i in range(j + 2)]
+        for i in range(j):
+            top = cos_list[i] * column[i] + sin_list[i] * column[i + 1]
+            column[i + 1] = -sin_list[i] * column[i] + cos_list[i] * column[i + 1]
+            column[i] = top
+        scale = lax.rsqrt(column[j] * column[j] + column[j + 1] * column[j + 1])
+        cos_now = column[j] * scale
+        sin_now = column[j + 1] * scale
+        rhs_g[j + 1] = -sin_now * rhs_g[j]
+        rhs_g[j] = cos_now * rhs_g[j]
+        cos_list.append(cos_now)
+        sin_list.append(sin_now)
+        upper.append(column[:j])
+        inverse.append(scale)
+    coeffs = [None] * steps
+    for j in range(steps - 1, -1, -1):
+        total = rhs_g[j]
+        for k in range(j + 1, steps):
+            total = total - upper[k][j] * coeffs[k]
+        coeffs[j] = total * inverse[j]
+    return coeffs
+
+
 def kernel(
     ns, nf,
     rf_hbm, rs_hbm, bl_hbm, we_hbm, kd_hbm, wf_ref, ws_ref, wc_hbm,
     xf_ref, xs_ref, ok_ref, wc,
     z, u, q, qm, bl, we, wm, kd, hs, hq, sq, he, wall, place, pairs, mpairs, scal, ra, rb,
-    tl, th, sb, pk, cb, ir, ib, blo, bhi, bs, pbs, wl, wh, wsr, pws, wn, pid, el, eh, es,
+    tl, th, lp, sb, pk, cb, ir, ib, wl, wh, wsr, pws, wn, pid, el, eh, es,
     in_sem, s_halo, r_halo, s_edge, r_edge, s_wall, r_wall, s_red, r_red, s_pair, r_pair, s_once, r_once,
 ):
     f32 = jnp.float32
@@ -271,14 +297,16 @@
             return remote(src, dst, s_pair.at[p, n], r_pair.at[p, n], to)
 
         return [
-            copy(0, z.at[k], tl.at[p], up),
-            copy(1, z.at[k], th.at[p], down),
-            copy(2, pk.at[p, :, pl.ds(4, 4)], sb.at[p, :, pl.ds(0, 4)], right),
-            copy(3, pk.at[p, :, pl.ds(0, 4)], sb.at[p, :, pl.ds(4, 4)], left),
+            copy(0, z.at[k, :, 1], tl.at[p, :, 1], up),
+            copy(1, z.at[k, :, 0], th.at[p, :, 0], down),
             copy(4, pk.at[p, :, pl.ds(5, 1)], cb.at[p, :, pl.ds(0, 1)], corners[0]),
             copy(5, pk.at[p, :, pl.ds(4, 1)], cb.at[p, :, pl.ds(1, 1)], corners[1]),
             copy(6, pk.at[p, :, pl.ds(1, 1)], cb.at[p, :, pl.ds(4, 1)], corners[2]),
             copy(7, pk.at[p, :, pl.ds(0, 1)], cb.at[p, :, pl.ds(5, 1)], corners[3]),
+            copy(12, lp.at[p, :, 1], tl.at[p, :, 0], up),
+            copy(13, lp.at[p, :, 0], th.at[p, :, 1], down),
+            copy(2, pk.at[p, :, pl.ds(4, 4)], sb.at[p, :, pl.ds(0, 4)], right),
+            copy(3, pk.at[p, :, pl.ds(0, 4)], sb.at[p, :, pl.ds(4, 4)], left),
         ]
 
     def inflow_copies(k):
@@ -291,54 +319,37 @@
             for n, to in enumerate((up, down, right, left))
         ]
 
-    def once_copies(chunk):
+    def once_copies():
         def copy(n, src, dst, to):
             return remote(src, dst, s_once.at[n], r_once.at[n], to)
 
-        low, high = CHUNKS[chunk]
-        rows = pl.ds(low, high - low)
         out = [
-            copy(2 * chunk, bl.at[rows, :, 1], blo.at[rows], up),
-            copy(2 * chunk + 1, bl.at[rows, :, 0], bhi.at[rows], down),
+            copy(0, we.at[:, 1], wl, up),
+            copy(1, we.at[:, 0], wh, down),
+            copy(2, pws.at[:, pl.ds(4, 4)], wsr.at[:, pl.ds(0, 4)], right),
+            copy(3, pws.at[:, pl.ds(0, 4)], wsr.at[:, pl.ds(4, 4)], left),
         ]
-        if chunk == 0:
-            n = 2 * len(CHUNKS)
-            out += [
-                copy(n, we.at[:, 1], wl, up),
-                copy(n + 1, we.at[:, 0], wh, down),
-                copy(n + 2, pbs.at[:, :, pl.ds(4, 2)], bs.at[:, :, pl.ds(0, 2)], right),
-                copy(n + 3, pbs.at[:, :, pl.ds(0, 2)], bs.at[:, :, pl.ds(4, 2)], left),
-                copy(n + 4, pws.at[:, pl.ds(4, 4)], wsr.at[:, pl.ds(0, 4)], right),
-                copy(n + 5, pws.at[:, pl.ds(0, 4)], wsr.at[:, pl.ds(4, 4)], left),
-            ]
-            out += [
-                copy(n + 6 + m, pid.at[pl.ds(4, 1)], pid.at[pl.ds(m, 1)], to)
-                for m, to in enumerate((up, down, right, left))
-            ]
-        return out
-
-    PACK = ((0, 0), (0, 1), (1, 0), (1, 1), (7, 0), (7, 1), (6, 0), (6, 1))
+        return out + [
+            copy(4 + m, pid.at[pl.ds(4, 1)], pid.at[pl.ds(m, 1)], to)
+            for m, to in enumerate((up, down, right, left))
+        ]
+
+    PACK = ((0, 0, 0), (1, 0, 1), (4, 7, 0), (5, 7, 1))
 
     def pack_once():
-        def one(i, c):
-            for g in range(6):
-                for m, (b, a) in enumerate(PACK):
-                    pbs[i, g, m : m + 1, :] = bl[i, g, a, b : b + 1, :]
-            for m, (b, a) in enumerate(PACK):
+        for i in range(6):
+            for m, b, a in PACK:
                 pws[i, m : m + 1, :] = we[i, a, b : b + 1, :]
-            return c
-
-        lax.fori_loop(0, 6, one, 0)
+                pws[i, m + 2 : m + 3, :] = we[i, a, b : b + 1, :]
         pid[4:5, :] = jnp.broadcast_to(patch.astype(f32), (1, 128))
 
     def prepare_pairs():
-        wn[0] = wl[2] * jnp.where(row8 == 0, has_left, 1.0)
-        wn[1] = wl[3] * jnp.where(row8 == 7, has_right, 1.0)
-        wn[2] = wh[2] * jnp.where(row8 == 0, has_left, 1.0)
-        wn[3] = wh[3] * jnp.where(row8 == 7, has_right, 1.0)
-        wn[4] = wsr[0] * jnp.where((row8 == 0) | (row8 == 4), has_down, 1.0)
-        wn[5] = wsr[1] * jnp.where((row8 == 1) | (row8 == 5), has_up, 1.0)
-        wn[6] = jnp.where(row8 < 4, wsr[2], wsr[3])
+        wn[0] = jnp.where(row8 == 0, has_left * wl[2], 0.0)
+        wn[1] = jnp.where(row8 == 7, has_right * wl[3], 0.0)
+        wn[2] = jnp.where(row8 == 0, has_left * wh[2], 0.0)
+        wn[3] = jnp.where(row8 == 7, has_right * wh[3], 0.0)
+        first = (row8 == 0) | (row8 == 4)
+        wn[4] = jnp.where(first, has_down * wsr[0], has_up * wsr[1])
         wn[7] = jnp.where(row8 < 4, wsr[3], wsr[2])
         here = row8.astype(f32)
         wn[8] = jnp.where(here + 8.0 == pid[0:1, :], 1.0, 0.0)
@@ -350,32 +361,16 @@
 
     def beside_cells(k):
         p = PAIRS.index(k)
-        odd = (row8 & 1) == 1
         for g in range(6):
-            v = tl[p, g, 1]
-            total = blo[g, 0] * tl[p, 0, 1]
-            for h in range(1, 6):
-                total = total + blo[g, h] * tl[p, h, 1]
-            total = total - wl[0] * tl[p, g, 0] - wl[1] * z[k, g, 0]
-            total = total - wn[0] * jnp.where(row8 == 0, cb[p, g, 0:1, :], pltpu.roll(v, 1, 0))
-            total = total - wn[1] * jnp.where(row8 == 7, cb[p, g, 4:5, :], pltpu.roll(v, 7, 0))
-            el[g] = total - wl[4] * pltpu.roll(v, 1, 1) - wl[5] * pltpu.roll(v, 127, 1)
-            v = th[p, g, 0]
-            total = bhi[g, 0] * th[p, 0, 0]
-            for h in range(1, 6):
-                total = total + bhi[g, h] * th[p, h, 0]
-            total = total - wh[0] * z[k, g, 1] - wh[1] * th[p, g, 1]
-            total = total - wn[2] * jnp.where(row8 == 0, cb[p, g, 1:2, :], pltpu.roll(v, 1, 0))
-            total = total - wn[3] * jnp.where(row8 == 7, cb[p, g, 5:6, :], pltpu.roll(v, 7, 0))
-            eh[g] = total - wh[4] * pltpu.roll(v, 1, 1) - wh[5] * pltpu.roll(v, 127, 1)
-            v = sb[p, g]
-            total = bs[g, 0] * sb[p, 0]
-            for h in range(1, 6):
-                total = total + bs[g, h] * sb[p, h]
-            total = total - wn[4] * jnp.where(odd, pltpu.roll(v, 1, 0), cb[p, g])
-            total = total - wn[5] * jnp.where(odd, cb[p, g], pltpu.roll(v, 7, 0))
-            total = total - wn[6] * pltpu.roll(v, 6, 0) - wn[7] * pk[p, g]
-            es[g] = total - wsr[4] * pltpu.roll(v, 1, 1) - wsr[5] * pltpu.roll(v, 127, 1)
+            el[g] = (
+                tl[p, g, 0] - wl[1] * z[k, g, 0]
+                - wn[0] * cb[p, g, 0:1, :] - wn[1] * cb[p, g, 4:5, :]
+            )
+            eh[g] = (
+                th[p, g, 1] - wh[0] * z[k, g, 1]
+                - wn[2] * cb[p, g, 1:2, :] - wn[3] * cb[p, g, 5:6, :]
+            )
+            es[g] = pltpu.roll(sb[p, g], 6, 0) - wn[4] * cb[p, g] - wn[7] * pk[p, g]
 
     def beside_inflow(k):
         p = PAIRS.index(k)
@@ -612,12 +607,12 @@
             else:
                 p = PAIRS.index(k)
                 copies = pair_copies(k)
-                copies[0].start()
-                copies[1].start()
+                for copy in copies[:2]:
+                    copy.start()
                 for g in range(6):
-                    for m, (b, a) in enumerate(PACK):
+                    for m, b, a in PACK:
                         pk[p, g, m : m + 1, :] = z[k, g, a, b : b + 1, :]
-                for copy in copies[4:] + copies[2:4]:
+                for copy in copies[2:6]:
                     copy.start()
         if step == when:
             early_gram()
@@ -625,10 +620,17 @@
         if k == 0:
             send_rows_flow(place, KRYLOV)
             pack_once()
-        if step < len(CHUNKS):
-            for copy in once_copies(step):
+            for copy in once_copies():
                 copy.start()
         local_part(k)
+        if width == 2:
+            for g in range(6):
+                for a in range(2):
+                    lp[p, g, a] = z[k + 1, g, a]
+                for m, b, a in PACK:
+                    pk[p, g, m + 2 : m + 3, :] = z[k + 1, g, a, b : b + 1, :]
+            for copy in copies[6:]:
+                copy.start()
         metal_step(k)
         if width == 2:
             p = PAIRS.index(k)
@@ -651,9 +653,8 @@
             )
         else:
             if k == PAIRS[0]:
-                for chunk in range(len(CHUNKS)):
-                    for copy in once_copies(chunk):
-                        copy.wait_recv()
+                for copy in once_copies():
+                    copy.wait_recv()
                 prepare_pairs()
             for copy in pair_copies(k):
                 copy.wait_recv()
@@ -701,9 +702,8 @@
     for k, width in PLAN:
         for copy in halos(k) if width == 1 else pair_copies(k) + inflow_copies(k):
             copy.wait_send()
-    for chunk in range(len(CHUNKS)):
-        for copy in once_copies(chunk):
-            copy.wait_send()
+    for copy in once_copies():
+        copy.wait_send()
     for k in range(KRYLOV):
         for copy in edges(k):
             copy.wait_send()
@@ -745,7 +745,7 @@
             if i <= j - 1:
                 t = t + r[i, j - 1] * coef_b[j]
             hess[i][j] = t
-    y = least_squares(hess, r[0, 0] / poly[0][0], zero, KRYLOV)
+    y = small_solve(hess, r[0, 0] / poly[0][0], zero, KRYLOV)
     top = jnp.abs(y[0])
     total = jnp.abs(y[0]) * spread[0]
     for k in range(1, KRYLOV):
@@ -765,6 +765,17 @@
             c = c + y[k] * poly[k][j]
         out = c * u[j] if out is None else out + c * u[j]
     xs_ref[...] = out
+
+
+def store(a_ref, b_ref, a_out, b_out, sem):
+    copies = [
+        pltpu.make_async_copy(a_ref, a_out, sem.at[0]),
+        pltpu.make_async_copy(b_ref, b_out, sem.at[1]),
+    ]
+    for copy in copies:
+        copy.start()
+    for copy in copies:
+        copy.wait()
 
 
 def shards(ns, nf, *args):
@@ -807,15 +818,12 @@
             pltpu.VMEM((2, 16, 128), f32),
             pltpu.VMEM((len(PAIRS), 6, 2, 8, 128), f32),
             pltpu.VMEM((len(PAIRS), 6, 2, 8, 128), f32),
+            pltpu.VMEM((len(PAIRS), 6, 2, 8, 128), f32),
             pltpu.VMEM((len(PAIRS), 6, 8, 128), f32),
             pltpu.VMEM((len(PAIRS), 6, 8, 128), f32),
             pltpu.VMEM((len(PAIRS), 6, 8, 128), f32),
             pltpu.VMEM((len(PAIRS), 8, 128), f32),
             pltpu.VMEM((len(PAIRS), 8, 128), f32),
-            pltpu.VMEM((6, 6, 8, 128), f32),
-            pltpu.VMEM((6, 6, 8, 128), f32),
-            pltpu.VMEM((6, 6, 8, 128), f32),
-            pltpu.VMEM((6, 6, 8, 128), f32),
             pltpu.VMEM((6, 8, 128), f32),
             pltpu.VMEM((6, 8, 128), f32),
             pltpu.VMEM((6, 8, 128), f32),
@@ -830,16 +838,27 @@
             dma((KRYLOV, 2)), dma((KRYLOV, 2)),
             dma((KRYLOV + 3,)), dma((KRYLOV + 3,)),
             dma((2,)), dma((2,)),
-            dma((len(PAIRS), 12)), dma((len(PAIRS), 12)),
-            dma((2 * len(CHUNKS) + 10,)), dma((2 * len(CHUNKS) + 10,)),
+            dma((len(PAIRS), 14)), dma((len(PAIRS), 14)),
+            dma((8,)), dma((8,)),
         ],
         compiler_params=pltpu.CompilerParams(
             collective_id=0, has_side_effects=True, vmem_limit_bytes=8 * 1024 * 1024
         ),
     )(*args)
-    return lax.cond(
-        ok[0, 0] > 0.5, lambda *a: (x_fluid, x_solid), lambda *a: arnoldi(*a), *args[:-1], coef
-    )
+    def place_out(*a):
+        return pl.pallas_call(
+            store,
+            name="place_out",
+            out_shape=(
+                jax.ShapeDtypeStruct(rhs_fluid.shape, f32),
+                jax.ShapeDtypeStruct(rhs_solid.shape, f32),
+            ),
+            in_specs=[vmem, vmem],
+            out_specs=(hbm, hbm),
+            scratch_shapes=[dma((2,))],
+        )(x_fluid, x_solid)
+
+    return lax.cond(ok[0, 0] > 0.5, place_out, lambda *a: arnoldi(*a), *args[:-1], coef)
 
 
 def solution(mesh):

time: 57.8 us -> 55.9 us (0.967)
  local copies, waits for them, and re-layouts: 1.88 us -> 0.66 us
  Pallas kernels: 53.6 us -> 52.7 us
    pallas_call x1, Pallas kernels: 53.6 us -> 52.1 us  [shards(): pl.pallas_call(functools.partial(kernel, ns, nf), name='gmres', out_shape...]
    unnamed x14 -> x12, local copies, waits for them, and re-layouts: 1.88 us -> 0.66 us
    pallas_call x0 -> x1, Pallas kernels: none -> 0.64 us  [place_out(): pl.pallas_call(store, name='place_out', out_shape=(jax.ShapeDtypeStruct(r...]
where the time goes in v5:
time: 55.9 us; the launch traced here: 55.7 us
  Pallas kernels  52.7 us (94%)
  between operations  2.28 us (4%)
  local copies, waits for them, and re-layouts  0.66 us (1%)
    pallas_call x1, Pallas kernels, shards(): pl.pallas_call(functools.partial(kernel, ns, nf), name='gmres', out_shape...  52.1 us

profile of v5, /device:TPU:1, one launch (start us, length us, event | category | flops | bytes accessed | tf_op | source)
XLA Modules:
  0.0 55.7 jit_solution(16385335826686891368)
XLA Ops:
  1.3 0.0 copy-start
  1.3 0.0 copy-start.2
  2.0 0.0 copy-done
  2.0 0.0 copy-start.1
  2.0 0.0 copy-start.4
  2.0 0.0 copy-start.5
  2.0 52.1 %gmres.1 = (f32[6,2,8,128]{3,2,1,0:T(8,128)S(1)}, f32[32,128]{1,0:T(8,128)S(1)}, f32[1,128]{1,0:T(1,128)S(1)}, f32[1,1,128]{2,1,0:T(1,128)S(1)}) custom-call(f32[6,2,8,128]{3,2,1,0:T(8,128)} %rf_hbm.1, f32[32,128]{1,0:T(8,128)} %rs_hbm.1, f32[6,6,2,8,128]{4,3,2,1,0:T(8,128)} %bl_hbm.1, f32[6,2,8,128]{3,2,1,0:T(8,128)} %we_hbm.1, f32[32,128]{1,0:T(8,128)} %kd_hbm.1, ...), custom_call_target="tpu_custom_call" | custom-call | tf_op jit(solution)/shard_map/gmres/pallas_call | solution.py:788
  54.1 0.0 copy-start.3
  54.2 0.0 copy-done.2
  54.2 0.0 copy-done.1
  54.2 0.0 copy-done.4
  54.2 0.0 copy-done.5
  54.2 0.6 %copy-done.3 = f32[32,128]{1,0:T(8,128)S(1)} copy-done((f32[32,128]{1,0:T(8,128)S(1)}, f32[32,128]{1,0:T(8,128)}, u32[]{:S(2)}) %copy-start.3) | copy-done | bytes 16408
  54.9 0.6 %conditional.1 = ((f32[6,2,8,128]{3,2,1,0:T(8,128)}, f32[32,128]{1,0:T(8,128)})) conditional(s32[]{:T(128)} %bitcast.98, (f32[6,2,8,128]{3,2,1,0:T(8,128)S(1)}, f32[32,128]{1,0:T(8,128)S(1)}, f32[6,6,2,8,128]{4,3,2,1,0:T(8,128)S(1)}, f32[6,2,8,128]{3,2,1,0:T(8,128)S(1)}, s32[1,1]{1,0:T(1,128)}, /*index=5*/f32[1,1,128]{2,1,0:T(1,128)S(1)}, ...), branch_computations={%region_0.76_spmd, %region_76.77_spmd} | conditional | flops 5884030 | bytes 15983141 | solution.py:861
  54.9 0.6 %place_out.1 = (f32[6,2,8,128]{3,2,1,0:T(8,128)}, f32[32,128]{1,0:T(8,128)}) custom-call(f32[6,2,8,128]{3,2,1,0:T(8,128)S(1)} %get-tuple-element.100.a_ref, f32[32,128]{1,0:T(8,128)S(1)} %get-tuple-element.101.b_ref), custom_call_target="tpu_custom_call" | custom-call | tf_op jit(solution)/shard_map/cond/branch_1_fun/place_out/pallas_call | solution.py:849
Async XLA Ops:
  1.3 0.7 %copy-start = (f32[1,1,128]{2,1,0:T(1,128)S(1)}, f32[1,1,128]{2,1,0:T(1,128)}, u32[]{:S(2)}) copy-start(f32[1,1,128]{2,1,0:T(1,128)} %wc_hbm.1) | copy-start | bytes 1540
  1.3 52.9 %copy-start.2 = (f32[6,6,2,8,128]{4,3,2,1,0:T(8,128)S(1)}, f32[6,6,2,8,128]{4,3,2,1,0:T(8,128)}, u32[]{:S(2)}) copy-start(f32[6,6,2,8,128]{4,3,2,1,0:T(8,128)} %bl_hbm.1) | copy-start | bytes 884740
  2.0 52.2 %copy-start.1 = (f32[6,2,8,128]{3,2,1,0:T(8,128)S(1)}, f32[6,2,8,128]{3,2,1,0:T(8,128)}, u32[]{:S(2)}) copy-start(f32[6,2,8,128]{3,2,1,0:T(8,128)} %rf_hbm.1) | copy-start | bytes 147460
  2.0 52.2 %copy-start.4 = (f32[32,128]{1,0:T(8,128)S(1)}, f32[32,128]{1,0:T(8,128)}, u32[]{:S(2)}) copy-start(f32[32,128]{1,0:T(8,128)} %kd_hbm.1) | copy-start | bytes 49156
  2.0 52.2 %copy-start.5 = (f32[6,2,8,128]{3,2,1,0:T(8,128)S(1)}, f32[6,2,8,128]{3,2,1,0:T(8,128)}, u32[]{:S(2)}) copy-start(f32[6,2,8,128]{3,2,1,0:T(8,128)} %we_hbm.1) | copy-start | bytes 147460
  54.1 0.7 %copy-start.3 = (f32[32,128]{1,0:T(8,128)S(1)}, f32[32,128]{1,0:T(8,128)}, u32[]{:S(2)}) copy-start(f32[32,128]{1,0:T(8,128)} %rs_hbm.1) | copy-start | bytes 49156

commit v6 on v5

--- a/solution.py
+++ b/solution.py
@@ -164,7 +164,7 @@
     ns, nf,
     rf_hbm, rs_hbm, bl_hbm, we_hbm, kd_hbm, wf_ref, ws_ref, wc_hbm,
     xf_ref, xs_ref, ok_ref, wc,
-    z, u, q, qm, bl, we, wm, kd, hs, hq, sq, he, wall, place, pairs, mpairs, scal, ra, rb,
+    z, u, q, qm, bl, we, wm, kd, hs, hq, sq, sinks, wall, place, pairs, mpairs, scal, ra, rb,
     tl, th, lp, sb, pk, cb, ir, ib, wl, wh, wsr, pws, wn, pid, el, eh, es,
     in_sem, s_halo, r_halo, s_edge, r_edge, s_wall, r_wall, s_red, r_red, s_pair, r_pair, s_once, r_once,
 ):
@@ -179,10 +179,10 @@
 
     loads = [
         pltpu.make_async_copy(rf_hbm, z.at[0], in_sem.at[0]),
-        pltpu.make_async_copy(rs_hbm, u.at[0], in_sem.at[1]),
+        pltpu.make_async_copy(rs_hbm, u.at[0, pl.ds(8, 32)], in_sem.at[1]),
         pltpu.make_async_copy(we_hbm, we, in_sem.at[2]),
         pltpu.make_async_copy(bl_hbm, bl, in_sem.at[3]),
-        pltpu.make_async_copy(kd_hbm, kd, in_sem.at[4]),
+        pltpu.make_async_copy(kd_hbm, kd.at[pl.ds(8, 32)], in_sem.at[4]),
         pltpu.make_async_copy(wc_hbm, wc, in_sem.at[5]),
     ]
     for load in loads:
@@ -220,6 +220,8 @@
     has_up = jnp.where(s < ns - 1, 1.0, 0.0).astype(f32)
     has_left = jnp.where(f > 0, 1.0, 0.0).astype(f32)
     has_right = jnp.where(f < nf - 1, 1.0, 0.0).astype(f32)
+    row48 = lax.broadcasted_iota(jnp.int32, (48, 128), 0)
+    inside = jnp.where(row48 < 8, has_down, jnp.where(row48 < 40, 1.0, has_up))
 
     def send_rows_flow(buf, k):
         for to in flow_peers:
@@ -261,17 +263,21 @@
             copy(3, sq.at[k, 1], hq.at[k, 1], left),
         ]
 
-    def edges(k):
-        def copy(n, src, dst, to):
+    def rows_to_bands(buf, n):
+        def copy(m, src, dst, to):
             return pltpu.make_async_remote_copy(
-                src_ref=src, dst_ref=dst, send_sem=s_edge.at[k, n], recv_sem=r_edge.at[k, n],
+                src_ref=buf.at[pl.ds(src, 8)], dst_ref=buf.at[pl.ds(dst, 8)],
+                send_sem=s_edge.at[n, m], recv_sem=r_edge.at[n, m],
                 device_id=to, device_id_type=MESH,
             )
 
-        return [
-            copy(0, u.at[k, pl.ds(31, 1)], he.at[k, 0, pl.ds(0, 1)], up),
-            copy(1, u.at[k, pl.ds(0, 1)], he.at[k, 1, pl.ds(0, 1)], down),
-        ]
+        return [copy(0, 32, 0, up), copy(1, 8, 40, down)]
+
+    def edges(k):
+        return rows_to_bands(sinks.at[k], k)
+
+    def first_edges():
+        return rows_to_bands(u.at[0], KRYLOV) + rows_to_bands(kd, KRYLOV + 1)
 
     def send_halos(k):
         out = halos(k)
@@ -414,9 +420,25 @@
     def metal_local(k):
         v = u[k]
         total = (4.0 + kd[...]) * v - pltpu.roll(v, 1, 1) - pltpu.roll(v, 127, 1)
-        below = jnp.where(row32 == 0, has_down * he[k, 0, 0:1, :], pltpu.roll(v, 1, 0))
-        above = jnp.where(row32 == 31, has_up * he[k, 1, 0:1, :], pltpu.roll(v, 31, 0))
-        return total - below - above
+        return (total - pltpu.roll(v, 1, 0) - pltpu.roll(v, 47, 0)) * inside
+
+    def metal_halo(k):
+        if k == 0:
+            for copy in first_edges():
+                copy.wait_recv()
+            u[0, 0:8, :] = u[0, 0:8, :] * has_down
+            u[0, 40:48, :] = u[0, 40:48, :] * has_up
+        else:
+            for copy in edges(k - 1):
+                copy.wait_recv()
+            u[k, 0:8, :] = u[k, 0:8, :] - has_down * sinks[k - 1, 0:8, :]
+            u[k, 40:48, :] = u[k, 40:48, :] - has_up * sinks[k - 1, 40:48, :]
+
+    def sink_of(k):
+        rows_flow(wall.at[k], k).wait_recv()
+        return jnp.dot(
+            state["pick"], wall[k], precision=lax.Precision.HIGHEST, preferred_element_type=f32
+        )
 
     def dot_row(store, i, j):
         total = store[i, 0, 0] * store[j, 0, 0] + store[i, 0, 1] * store[j, 0, 1]
@@ -448,8 +470,6 @@
     for copy in halos(0):
         copy.start()
     loads[1].wait()
-    for copy in edges(0):
-        copy.start()
     pairs[...] = jnp.zeros((32, 128), f32)
     mpairs[...] = jnp.zeros((32, 128), f32)
     loads[2].wait()
@@ -461,6 +481,8 @@
     wm[4, 1] = has_up * we[1, 1]
     loads[3].wait()
     loads[4].wait()
+    for copy in first_edges():
+        copy.start()
 
     own = []
     state = {}
@@ -475,17 +497,13 @@
             places = jnp.sum(place[...], axis=0, keepdims=True)
             state["pick"] = jnp.where((row32.astype(f32) == places) & (lane32 < 32), 1.0, 0.0)[:, 0:32]
         if k > 0:
-            rows_flow(wall.at[k - 1], k - 1).wait_recv()
-            sink = jnp.dot(
-                state["pick"], wall[k - 1],
-                precision=lax.Precision.HIGHEST, preferred_element_type=f32,
-            )
+            metal_halo(k - 1)
+            u[k] = metal_local(k - 1)
+            sinks[k - 1, 8:40, :] = sink_of(k - 1)
             for copy in edges(k - 1):
-                copy.wait_recv()
-            u[k] = metal_local(k - 1) - sink
-            for copy in edges(k):
                 copy.start()
-        own.append(own_metal(u[k]))
+            u[k, 8:40, :] = u[k, 8:40, :] - sinks[k - 1, 8:40, :]
+        own.append(own_metal(u[k, 8:40, :]))
 
     def early_gram():
         n = 0
@@ -580,7 +598,8 @@
         for i in range(low, KRYLOV + 1):
             t = None if first else qm[i]
             for j in range(low, min(i, high) + 1):
-                t = poly[i][j] * u[j] if t is None else t + poly[i][j] * u[j]
+                rows = u[j, 8:40, :]
+                t = poly[i][j] * rows if t is None else t + poly[i][j] * rows
             qm[i] = t
 
     def place_of(j, i):
@@ -687,13 +706,9 @@
     coef_a, coef_b, poly, spread = state["basis"]
     metal_combine(0, last - 1, True)
     metal_gram_rows(0, last - 1)
-    rows_flow(wall.at[last - 1], last - 1).wait_recv()
-    sink = jnp.dot(
-        state["pick"], wall[last - 1], precision=lax.Precision.HIGHEST, preferred_element_type=f32
-    )
-    for copy in edges(last - 1):
-        copy.wait_recv()
-    qm[last] = qm[last] + poly[last][last] * (metal_local(last - 1) - sink)
+    metal_halo(last - 1)
+    rows = metal_local(last - 1)[8:40, :] - sink_of(last - 1)
+    qm[last] = qm[last] + poly[last][last] * rows
     metal_gram_rows(last, last)
     metal_done = packed(mpairs, 0, 32)
     rows_flow(ra.at[1], KRYLOV + 2).wait_recv()
@@ -704,7 +719,9 @@
             copy.wait_send()
     for copy in once_copies():
         copy.wait_send()
-    for k in range(KRYLOV):
+    for copy in first_edges():
+        copy.wait_send()
+    for k in range(KRYLOV - 1):
         for copy in edges(k):
             copy.wait_send()
     for k in range(KRYLOV):
@@ -763,7 +780,7 @@
         c = y[j] * poly[j][j]
         for k in range(j + 1, KRYLOV):
             c = c + y[k] * poly[k][j]
-        out = c * u[j] if out is None else out + c * u[j]
+        out = c * u[j, 8:40, :] if out is None else out + c * u[j, 8:40, :]
     xs_ref[...] = out
 
 
@@ -798,17 +815,17 @@
         out_specs=(vmem,) * 4,
         scratch_shapes=[
             pltpu.VMEM((KRYLOV + 1, 6, 2, 8, 128), f32),
-            pltpu.VMEM((KRYLOV, 32, 128), f32),
+            pltpu.VMEM((KRYLOV, 48, 128), f32),
             pltpu.VMEM((KRYLOV + 1, 6, 2, 8, 128), f32),
             pltpu.VMEM((KRYLOV + 1, 32, 128), f32),
             pltpu.VMEM((6, 6, 2, 8, 128), f32),
             pltpu.VMEM((6, 2, 8, 128), f32),
             pltpu.VMEM((5, 2, 8, 128), f32),
-            pltpu.VMEM((32, 128), f32),
+            pltpu.VMEM((48, 128), f32),
             pltpu.VMEM((KRYLOV, 2, 6, 8, 128), f32),
             pltpu.VMEM((KRYLOV, 2, 16, 128), f32),
             pltpu.VMEM((KRYLOV, 2, 16, 128), f32),
-            pltpu.VMEM((KRYLOV, 2, 8, 128), f32),
+            pltpu.VMEM((KRYLOV - 1, 48, 128), f32),
             pltpu.VMEM((KRYLOV, 32, 128), f32),
             pltpu.VMEM((32, 128), f32),
             pltpu.VMEM((32, 128), f32),
@@ -835,7 +852,7 @@
             pltpu.VMEM((6, 8, 128), f32),
             dma((6,)),
             dma((KRYLOV, 4)), dma((KRYLOV, 4)),
-            dma((KRYLOV, 2)), dma((KRYLOV, 2)),
+            dma((KRYLOV + 2, 2)), dma((KRYLOV + 2, 2)),
             dma((KRYLOV + 3,)), dma((KRYLOV + 3,)),
             dma((2,)), dma((2,)),
             dma((len(PAIRS), 14)), dma((len(PAIRS), 14)),

time: 55.9 us -> 56.2 us (level)
  no operation moved by 1% of the time
where the time goes in v6:
time: 56.2 us; the launch traced here: 55.9 us
  Pallas kernels  53 us (94%)
  between operations  2.28 us (4%)
  local copies, waits for them, and re-layouts  0.66 us (1%)
    pallas_call x1, Pallas kernels, shards(): pl.pallas_call(functools.partial(kernel, ns, nf), name='gmres', out_shape...  52.4 us

profile of v6, /device:TPU:1, one launch (start us, length us, event | category | flops | bytes accessed | tf_op | source)
XLA Modules:
  0.0 55.9 jit_solution(6967227845127889770)
XLA Ops:
  1.3 0.0 copy-start
  1.3 0.0 copy-start.2
  2.0 0.0 copy-done
  2.0 0.0 copy-start.1
  2.0 0.0 copy-start.4
  2.0 0.0 copy-start.5
  2.0 52.4 %gmres.1 = (f32[6,2,8,128]{3,2,1,0:T(8,128)S(1)}, f32[32,128]{1,0:T(8,128)S(1)}, f32[1,128]{1,0:T(1,128)S(1)}, f32[1,1,128]{2,1,0:T(1,128)S(1)}) custom-call(f32[6,2,8,128]{3,2,1,0:T(8,128)} %rf_hbm.1, f32[32,128]{1,0:T(8,128)} %rs_hbm.1, f32[6,6,2,8,128]{4,3,2,1,0:T(8,128)} %bl_hbm.1, f32[6,2,8,128]{3,2,1,0:T(8,128)} %we_hbm.1, f32[32,128]{1,0:T(8,128)} %kd_hbm.1, ...), custom_call_target="tpu_custom_call" | custom-call | tf_op jit(solution)/shard_map/gmres/pallas_call | solution.py:805
  54.4 0.0 copy-start.3
  54.4 0.0 copy-done.2
  54.4 0.0 copy-done.1
  54.5 0.0 copy-done.4
  54.5 0.0 copy-done.5
  54.5 0.6 %copy-done.3 = f32[32,128]{1,0:T(8,128)S(1)} copy-done((f32[32,128]{1,0:T(8,128)S(1)}, f32[32,128]{1,0:T(8,128)}, u32[]{:S(2)}) %copy-start.3) | copy-done | bytes 16408
  55.1 0.6 %conditional.1 = ((f32[6,2,8,128]{3,2,1,0:T(8,128)}, f32[32,128]{1,0:T(8,128)})) conditional(s32[]{:T(128)} %bitcast.98, (f32[6,2,8,128]{3,2,1,0:T(8,128)S(1)}, f32[32,128]{1,0:T(8,128)S(1)}, f32[6,6,2,8,128]{4,3,2,1,0:T(8,128)S(1)}, f32[6,2,8,128]{3,2,1,0:T(8,128)S(1)}, s32[1,1]{1,0:T(1,128)}, /*index=5*/f32[1,1,128]{2,1,0:T(1,128)S(1)}, ...), branch_computations={%region_0.76_spmd, %region_76.77_spmd} | conditional | flops 5884030 | bytes 15983141 | solution.py:878
  55.1 0.6 %place_out.1 = (f32[6,2,8,128]{3,2,1,0:T(8,128)}, f32[32,128]{1,0:T(8,128)}) custom-call(f32[6,2,8,128]{3,2,1,0:T(8,128)S(1)} %get-tuple-element.100.a_ref, f32[32,128]{1,0:T(8,128)S(1)} %get-tuple-element.101.b_ref), custom_call_target="tpu_custom_call" | custom-call | tf_op jit(solution)/shard_map/cond/branch_1_fun/place_out/pallas_call | solution.py:866
Async XLA Ops:
  1.3 0.7 %copy-start = (f32[1,1,128]{2,1,0:T(1,128)S(1)}, f32[1,1,128]{2,1,0:T(1,128)}, u32[]{:S(2)}) copy-start(f32[1,1,128]{2,1,0:T(1,128)} %wc_hbm.1) | copy-start | bytes 1540
  1.3 53.2 %copy-start.2 = (f32[6,6,2,8,128]{4,3,2,1,0:T(8,128)S(1)}, f32[6,6,2,8,128]{4,3,2,1,0:T(8,128)}, u32[]{:S(2)}) copy-start(f32[6,6,2,8,128]{4,3,2,1,0:T(8,128)} %bl_hbm.1) | copy-start | bytes 884740
  2.0 52.5 %copy-start.1 = (f32[6,2,8,128]{3,2,1,0:T(8,128)S(1)}, f32[6,2,8,128]{3,2,1,0:T(8,128)}, u32[]{:S(2)}) copy-start(f32[6,2,8,128]{3,2,1,0:T(8,128)} %rf_hbm.1) | copy-start | bytes 147460
  2.0 52.5 %copy-start.4 = (f32[32,128]{1,0:T(8,128)S(1)}, f32[32,128]{1,0:T(8,128)}, u32[]{:S(2)}) copy-start(f32[32,128]{1,0:T(8,128)} %kd_hbm.1) | copy-start | bytes 49156
  2.0 52.5 %copy-start.5 = (f32[6,2,8,128]{3,2,1,0:T(8,128)S(1)}, f32[6,2,8,128]{3,2,1,0:T(8,128)}, u32[]{:S(2)}) copy-start(f32[6,2,8,128]{3,2,1,0:T(8,128)} %we_hbm.1) | copy-start | bytes 147460
  54.4 0.7 %copy-start.3 = (f32[32,128]{1,0:T(8,128)S(1)}, f32[32,128]{1,0:T(8,128)}, u32[]{:S(2)}) copy-start(f32[32,128]{1,0:T(8,128)} %rs_hbm.1) | copy-start | bytes 49156

commit v7 on v6

--- a/solution.py
+++ b/solution.py
@@ -10,7 +10,7 @@
 KRYLOV = 6
 MESH = pl.DeviceIdType.MESH
 EARLY = 2
-PLAN = ((0, 1), (1, 1), (2, 1), (3, 1), (4, 2))
+PLAN = ((0, 2), (2, 1), (3, 1), (4, 2))
 PAIRS = tuple(k for k, width in PLAN if width == 2)
 
 
@@ -467,8 +467,9 @@
             sq[0, 1, i : i + 1, :] = z[0, g, a, 0:1, :]
     sq[:, :, 12:16, :] = jnp.zeros((KRYLOV, 2, 4, 128), f32)
     pl.semaphore_wait(barrier, ns + nf + 2)
-    for copy in halos(0):
-        copy.start()
+    if PLAN[0][1] == 1:
+        for copy in halos(0):
+            copy.start()
     loads[1].wait()
     pairs[...] = jnp.zeros((32, 128), f32)
     mpairs[...] = jnp.zeros((32, 128), f32)
@@ -620,19 +621,18 @@
     early = [k for k, _ in PLAN if k >= EARLY - 1][0]
     when = [k for k, _ in PLAN].index(early)
     for step, (k, width) in enumerate(PLAN):
-        if k > 0:
-            if width == 1:
-                send_halos(k)
-            else:
-                p = PAIRS.index(k)
-                copies = pair_copies(k)
-                for copy in copies[:2]:
-                    copy.start()
-                for g in range(6):
-                    for m, b, a in PACK:
-                        pk[p, g, m : m + 1, :] = z[k, g, a, b : b + 1, :]
-                for copy in copies[2:6]:
-                    copy.start()
+        if width == 2:
+            p = PAIRS.index(k)
+            copies = pair_copies(k)
+            for copy in copies[:2]:
+                copy.start()
+            for g in range(6):
+                for m, b, a in PACK:
+                    pk[p, g, m : m + 1, :] = z[k, g, a, b : b + 1, :]
+            for copy in copies[2:6]:
+                copy.start()
+        elif k > 0:
+            send_halos(k)
         if step == when:
             early_gram()
         wall_step(k)
@@ -658,7 +658,7 @@
                 copy.start()
         if step == when + 1:
             early_span()
-        if step == when + 3:
+        if step == len(PLAN) - 1:
             state["basis"] = basis()
             combine(0, k, True)
             gram_rows(0, k)

time: 56.2 us -> 58.1 us (1.034)
  Pallas kernels: 53 us -> 54.9 us
    pallas_call x1, Pallas kernels: 52.4 us -> 54.3 us  [shards(): pl.pallas_call(functools.partial(kernel, ns, nf), name='gmres', out_shape...]
where the time goes in v7:
time: 58.1 us; the launch traced here: 57.8 us
  Pallas kernels  54.9 us (94%)
  between operations  2.28 us (4%)
  local copies, waits for them, and re-layouts  0.66 us (1%)
    pallas_call x1, Pallas kernels, shards(): pl.pallas_call(functools.partial(kernel, ns, nf), name='gmres', out_shape...  54.3 us

profile of v7, /device:TPU:1, one launch (start us, length us, event | category | flops | bytes accessed | tf_op | source)
XLA Modules:
  0.0 57.8 jit_solution(4780132980538008860)
XLA Ops:
  1.3 0.0 copy-start
  1.3 0.0 copy-start.2
  2.0 0.0 copy-done
  2.0 0.0 copy-start.1
  2.0 0.0 copy-start.4
  2.0 0.0 copy-start.5
  2.0 54.3 %gmres.1 = (f32[6,2,8,128]{3,2,1,0:T(8,128)S(1)}, f32[32,128]{1,0:T(8,128)S(1)}, f32[1,128]{1,0:T(1,128)S(1)}, f32[1,1,128]{2,1,0:T(1,128)S(1)}) custom-call(f32[6,2,8,128]{3,2,1,0:T(8,128)} %rf_hbm.1, f32[32,128]{1,0:T(8,128)} %rs_hbm.1, f32[6,6,2,8,128]{4,3,2,1,0:T(8,128)} %bl_hbm.1, f32[6,2,8,128]{3,2,1,0:T(8,128)} %we_hbm.1, f32[32,128]{1,0:T(8,128)} %kd_hbm.1, ...), custom_call_target="tpu_custom_call" | custom-call | tf_op jit(solution)/shard_map/gmres/pallas_call | solution.py:805
  56.3 0.0 copy-start.3
  56.3 0.0 copy-done.2
  56.4 0.0 copy-done.1
  56.4 0.0 copy-done.4
  56.4 0.0 copy-done.5
  56.4 0.6 %copy-done.3 = f32[32,128]{1,0:T(8,128)S(1)} copy-done((f32[32,128]{1,0:T(8,128)S(1)}, f32[32,128]{1,0:T(8,128)}, u32[]{:S(2)}) %copy-start.3) | copy-done | bytes 16408
  57.0 0.6 %conditional.1 = ((f32[6,2,8,128]{3,2,1,0:T(8,128)}, f32[32,128]{1,0:T(8,128)})) conditional(s32[]{:T(128)} %bitcast.98, (f32[6,2,8,128]{3,2,1,0:T(8,128)S(1)}, f32[32,128]{1,0:T(8,128)S(1)}, f32[6,6,2,8,128]{4,3,2,1,0:T(8,128)S(1)}, f32[6,2,8,128]{3,2,1,0:T(8,128)S(1)}, s32[1,1]{1,0:T(1,128)}, /*index=5*/f32[1,1,128]{2,1,0:T(1,128)S(1)}, ...), branch_computations={%region_0.76_spmd, %region_76.77_spmd} | conditional | flops 5884030 | bytes 15983141 | solution.py:878
  57.0 0.6 %place_out.1 = (f32[6,2,8,128]{3,2,1,0:T(8,128)}, f32[32,128]{1,0:T(8,128)}) custom-call(f32[6,2,8,128]{3,2,1,0:T(8,128)S(1)} %get-tuple-element.100.a_ref, f32[32,128]{1,0:T(8,128)S(1)} %get-tuple-element.101.b_ref), custom_call_target="tpu_custom_call" | custom-call | tf_op jit(solution)/shard_map/cond/branch_1_fun/place_out/pallas_call | solution.py:866
Async XLA Ops:
  1.3 0.7 %copy-start = (f32[1,1,128]{2,1,0:T(1,128)S(1)}, f32[1,1,128]{2,1,0:T(1,128)}, u32[]{:S(2)}) copy-start(f32[1,1,128]{2,1,0:T(1,128)} %wc_hbm.1) | copy-start | bytes 1540
  1.3 55.1 %copy-start.2 = (f32[6,6,2,8,128]{4,3,2,1,0:T(8,128)S(1)}, f32[6,6,2,8,128]{4,3,2,1,0:T(8,128)}, u32[]{:S(2)}) copy-start(f32[6,6,2,8,128]{4,3,2,1,0:T(8,128)} %bl_hbm.1) | copy-start | bytes 884740
  2.0 54.4 %copy-start.1 = (f32[6,2,8,128]{3,2,1,0:T(8,128)S(1)}, f32[6,2,8,128]{3,2,1,0:T(8,128)}, u32[]{:S(2)}) copy-start(f32[6,2,8,128]{3,2,1,0:T(8,128)} %rf_hbm.1) | copy-start | bytes 147460
  2.0 54.4 %copy-start.4 = (f32[32,128]{1,0:T(8,128)S(1)}, f32[32,128]{1,0:T(8,128)}, u32[]{:S(2)}) copy-start(f32[32,128]{1,0:T(8,128)} %kd_hbm.1) | copy-start | bytes 49156
  2.0 54.4 %copy-start.5 = (f32[6,2,8,128]{3,2,1,0:T(8,128)S(1)}, f32[6,2,8,128]{3,2,1,0:T(8,128)}, u32[]{:S(2)}) copy-start(f32[6,2,8,128]{3,2,1,0:T(8,128)} %we_hbm.1) | copy-start | bytes 147460
  56.3 0.7 %copy-start.3 = (f32[32,128]{1,0:T(8,128)S(1)}, f32[32,128]{1,0:T(8,128)}, u32[]{:S(2)}) copy-start(f32[32,128]{1,0:T(8,128)} %rs_hbm.1) | copy-start | bytes 49156

commit v8 on v6

--- a/solution.py
+++ b/solution.py
@@ -497,11 +497,11 @@
             places = jnp.sum(place[...], axis=0, keepdims=True)
             state["pick"] = jnp.where((row32.astype(f32) == places) & (lane32 < 32), 1.0, 0.0)[:, 0:32]
         if k > 0:
-            metal_halo(k - 1)
-            u[k] = metal_local(k - 1)
             sinks[k - 1, 8:40, :] = sink_of(k - 1)
             for copy in edges(k - 1):
                 copy.start()
+            metal_halo(k - 1)
+            u[k] = metal_local(k - 1)
             u[k, 8:40, :] = u[k, 8:40, :] - sinks[k - 1, 8:40, :]
         own.append(own_metal(u[k, 8:40, :]))
 

time: 56.2 us -> 56 us (level)
  no operation moved by 1% of the time
where the time goes in v8:
time: 56 us; the launch traced here: 55.8 us
  Pallas kernels  52.9 us (94%)
  between operations  2.28 us (4%)
  local copies, waits for them, and re-layouts  0.66 us (1%)
    pallas_call x1, Pallas kernels, shards(): pl.pallas_call(functools.partial(kernel, ns, nf), name='gmres', out_shape...  52.2 us

profile of v8, /device:TPU:1, one launch (start us, length us, event | category | flops | bytes accessed | tf_op | source)
XLA Modules:
  0.0 55.8 jit_solution(6682222113446033031)
XLA Ops:
  1.3 0.0 copy-start
  1.3 0.0 copy-start.2
  2.0 0.0 copy-done
  2.0 0.0 copy-start.1
  2.0 0.0 copy-start.4
  2.0 0.0 copy-start.5
  2.0 52.2 %gmres.1 = (f32[6,2,8,128]{3,2,1,0:T(8,128)S(1)}, f32[32,128]{1,0:T(8,128)S(1)}, f32[1,128]{1,0:T(1,128)S(1)}, f32[1,1,128]{2,1,0:T(1,128)S(1)}) custom-call(f32[6,2,8,128]{3,2,1,0:T(8,128)} %rf_hbm.1, f32[32,128]{1,0:T(8,128)} %rs_hbm.1, f32[6,6,2,8,128]{4,3,2,1,0:T(8,128)} %bl_hbm.1, f32[6,2,8,128]{3,2,1,0:T(8,128)} %we_hbm.1, f32[32,128]{1,0:T(8,128)} %kd_hbm.1, ...), custom_call_target="tpu_custom_call" | custom-call | tf_op jit(solution)/shard_map/gmres/pallas_call | solution.py:805
  54.3 0.0 copy-start.3
  54.3 0.0 copy-done.2
  54.3 0.0 copy-done.1
  54.3 0.0 copy-done.4
  54.3 0.0 copy-done.5
  54.4 0.6 %copy-done.3 = f32[32,128]{1,0:T(8,128)S(1)} copy-done((f32[32,128]{1,0:T(8,128)S(1)}, f32[32,128]{1,0:T(8,128)}, u32[]{:S(2)}) %copy-start.3) | copy-done | bytes 16408
  55.0 0.6 %conditional.1 = ((f32[6,2,8,128]{3,2,1,0:T(8,128)}, f32[32,128]{1,0:T(8,128)})) conditional(s32[]{:T(128)} %bitcast.98, (f32[6,2,8,128]{3,2,1,0:T(8,128)S(1)}, f32[32,128]{1,0:T(8,128)S(1)}, f32[6,6,2,8,128]{4,3,2,1,0:T(8,128)S(1)}, f32[6,2,8,128]{3,2,1,0:T(8,128)S(1)}, s32[1,1]{1,0:T(1,128)}, /*index=5*/f32[1,1,128]{2,1,0:T(1,128)S(1)}, ...), branch_computations={%region_0.76_spmd, %region_76.77_spmd} | conditional | flops 5884030 | bytes 15983141 | solution.py:878
  55.0 0.6 %place_out.1 = (f32[6,2,8,128]{3,2,1,0:T(8,128)}, f32[32,128]{1,0:T(8,128)}) custom-call(f32[6,2,8,128]{3,2,1,0:T(8,128)S(1)} %get-tuple-element.100.a_ref, f32[32,128]{1,0:T(8,128)S(1)} %get-tuple-element.101.b_ref), custom_call_target="tpu_custom_call" | custom-call | tf_op jit(solution)/shard_map/cond/branch_1_fun/place_out/pallas_call | solution.py:866
Async XLA Ops:
  1.3 0.7 %copy-start = (f32[1,1,128]{2,1,0:T(1,128)S(1)}, f32[1,1,128]{2,1,0:T(1,128)}, u32[]{:S(2)}) copy-start(f32[1,1,128]{2,1,0:T(1,128)} %wc_hbm.1) | copy-start | bytes 1540
  1.3 53.0 %copy-start.2 = (f32[6,6,2,8,128]{4,3,2,1,0:T(8,128)S(1)}, f32[6,6,2,8,128]{4,3,2,1,0:T(8,128)}, u32[]{:S(2)}) copy-start(f32[6,6,2,8,128]{4,3,2,1,0:T(8,128)} %bl_hbm.1) | copy-start | bytes 884740
  2.0 52.3 %copy-start.1 = (f32[6,2,8,128]{3,2,1,0:T(8,128)S(1)}, f32[6,2,8,128]{3,2,1,0:T(8,128)}, u32[]{:S(2)}) copy-start(f32[6,2,8,128]{3,2,1,0:T(8,128)} %rf_hbm.1) | copy-start | bytes 147460
  2.0 52.3 %copy-start.4 = (f32[32,128]{1,0:T(8,128)S(1)}, f32[32,128]{1,0:T(8,128)}, u32[]{:S(2)}) copy-start(f32[32,128]{1,0:T(8,128)} %kd_hbm.1) | copy-start | bytes 49156
  2.0 52.3 %copy-start.5 = (f32[6,2,8,128]{3,2,1,0:T(8,128)S(1)}, f32[6,2,8,128]{3,2,1,0:T(8,128)}, u32[]{:S(2)}) copy-start(f32[6,2,8,128]{3,2,1,0:T(8,128)} %we_hbm.1) | copy-start | bytes 147460
  54.3 0.7 %copy-start.3 = (f32[32,128]{1,0:T(8,128)S(1)}, f32[32,128]{1,0:T(8,128)}, u32[]{:S(2)}) copy-start(f32[32,128]{1,0:T(8,128)} %rs_hbm.1) | copy-start | bytes 49156
